TPU v7x, 32 devices: a whole 2x2x4 slice. The times are simulated.
32 devices in a mesh: grp: 2 (over x), seq: 16 (over z, y, core).
Axes of the slice: x: 2, y: 2, z: 4, core: 2. Of those that a mesh axis runs over, the one named last changes fastest.
Arguments:
- projected: bfloat16 [3, 4096, 4096], P(None, ('grp', 'seq')), parts along dimension 1, may hold values from -6 to 6
- short_taps: float32 [3, 3, 4096], replicated, may hold values from -3 to 3
- skip_gain: float32 [4096], replicated, may hold values from -3 to 3
- residues: float32 [2, 2, 4096], replicated, may hold values from -0.125 to 0.125
- pole_angles: float32 [2, 4096], replicated, may hold values from -3.140625 to 3.140625
- decay_rates: float32 [2, 4096], replicated, may hold values from 3.0517578e-05 to 0.03125
Outputs:
- gated: bfloat16 [4096, 4096], P(('grp', 'seq')), parts along dimension 0
There are 2 independent parts, one for each index of `grp`. A program takes and returns all parts, laid end to end along the dimension named above; an argument that names none is the same for every part. Nothing has to cross between parts.
All inputs are finite; a program needn't handle non-finite values.
Results may differ from a plain program's by a relative error of at most 0.008.
Values may be sent and summed in bfloat16 or wider, within the bound.
A program may use at most 128 MiB of HBM per device.

v0:
```python
import functools

import jax
import jax.numpy as jnp
from jax import lax
from jax.experimental import pallas as pl
from jax.experimental.pallas import tpu as pltpu
from jax.sharding import PartitionSpec as P

MESH = pl.DeviceIdType.MESH
LANES = 128
CHUNKS = 8
WIDE = 256
F32 = jnp.float32
BF16 = jnp.bfloat16

RE1, IM1, C1, C2, RE16, IM16, RE32, IM32, RE64, IM64, RE128, IM128, G0, G1, H1, H0R, H0I = range(17)
TABLE_ROWS = 17


def square(re, im):
    return re * re - im * im, 2.0 * (re * im)


def cos_sin_half(angle):
    x = 0.5 * angle
    z = x * x
    s = 1.0 / 6227020800.0
    for coefficient in (-1.0 / 39916800.0, 1.0 / 362880.0, -1.0 / 5040.0, 1.0 / 120.0, -1.0 / 6.0, 1.0):
        s = s * z + coefficient
    c = -1.0 / 87178291200.0
    for coefficient in (1.0 / 479001600.0, -1.0 / 3628800.0, 1.0 / 40320.0, -1.0 / 720.0, 1.0 / 24.0, -0.5, 1.0):
        c = c * z + coefficient
    return c, s * x


def kernel(
    n, owners, per_owner,
    x_hbm, taps_hbm, skip_hbm, res_hbm, ang_hbm, dec_hbm, out_hbm,
    xs, tail, taps, skip, res, ang, dec, to_chunks, to_rows, tab,
    halo_f32, halo_send, halo_recv, halo,
    prod, local, query, scan, t_send, t_in, c_out, c_in, rot_a, rot_b, outs,
    in_sems, kv_sems, out_sems, halo_sems, t_ssem, t_rsem, c_ssem, c_rsem,
):
    rows, width = xs.shape[1], xs.shape[2]
    steps = rows // CHUNKS
    half_width = width // 2
    blocks = width // WIDE
    kv_parts = kv_sems.shape[0]
    part_width = width // kv_parts
    msg_rows = t_send.shape[1]
    half_msg = msg_rows // 2
    me = lax.axis_index("seq")

    barrier = pltpu.get_barrier_semaphore()

    def greet(d, carry):
        pl.semaphore_signal(
            barrier, inc=1, device_id={"seq": lax.rem(me + d, n)}, device_id_type=MESH
        )
        return carry

    def kv_copy(part):
        cols = pl.ds(pl.multiple_of(part * part_width, part_width), part_width)
        return pltpu.make_async_copy(
            x_hbm.at[pl.ds(1, 2), :, cols], xs.at[pl.ds(1, 2), :, cols], kv_sems.at[part]
        )

    tail_copy = pltpu.make_async_copy(
        x_hbm.at[:, pl.ds(rows - 16, 16), :], tail, in_sems.at[0]
    )
    tail_copy.start()
    small = [
        pltpu.make_async_copy(source, target, in_sems.at[1 + i])
        for i, (source, target) in enumerate(
            [(ang_hbm, ang), (dec_hbm, dec), (res_hbm, res), (taps_hbm, taps), (skip_hbm, skip)]
        )
    ]
    for copy in small:
        copy.start()
    for part in range(kv_parts):
        kv_copy(part).start()
    q_copy = pltpu.make_async_copy(x_hbm.at[0], xs.at[0], in_sems.at[6])
    q_copy.start()
    lax.fori_loop(1, n, greet, 0)

    i0 = lax.broadcasted_iota(jnp.int32, (rows, rows), 0)
    i1 = lax.broadcasted_iota(jnp.int32, (rows, rows), 1)
    to_chunks[...] = jnp.where(i1 == (i0 % CHUNKS) * steps + i0 // CHUNKS, 1.0, 0.0).astype(BF16)
    to_rows[...] = jnp.where(i0 == (i1 % CHUNKS) * steps + i1 // CHUNKS, 1.0, 0.0).astype(BF16)

    tail_copy.wait()
    for i in range(3):
        last = tail[i].astype(F32)[14:16]
        halo_f32[2 * i : 2 * i + 2, :] = last[:, :half_width]
        halo_f32[8 + 2 * i : 10 + 2 * i, :] = last[:, half_width:]
    halo_f32[6:8, :] = jnp.zeros((2, half_width), F32)
    halo_f32[14:16, :] = jnp.zeros((2, half_width), F32)
    halo_send[...] = halo_f32[...].astype(BF16)
    halo_copy = pltpu.make_async_remote_copy(
        src_ref=halo_send,
        dst_ref=halo_recv,
        send_sem=halo_sems.at[0],
        recv_sem=halo_sems.at[1],
        device_id={"seq": lax.rem(me + 1, n)},
        device_id_type=MESH,
    )
    pl.semaphore_wait(barrier, n - 1)
    pl.when(me < n - 1)(halo_copy.start)

    for copy in small:
        copy.wait()

    def parameters(b, carry):
        cols = pl.ds(pl.multiple_of(b * WIDE, WIDE), WIDE)
        c, s = cos_sin_half(ang[:, cols])
        root = jnp.exp(-0.5 * dec[:, cols])
        re, im = square(root * c, root * s)
        r0, r1 = res[0, :, cols], res[1, :, cols]
        tab[RE1, :, cols] = re
        tab[IM1, :, cols] = im
        tab[C1, :, cols] = 2.0 * re
        tab[C2, :, cols] = -(re * re + im * im)
        tab[G0, :, cols] = r0
        tab[G1, :, cols] = -(r0 * re + r1 * im)
        tab[H1, :, cols] = -r1
        tab[H0R, :, cols] = r0 * re - r1 * im
        tab[H0I, :, cols] = -(r0 * im + r1 * re)
        power = 1
        while power < rows:
            re, im = square(re, im)
            power *= 2
            if power == steps:
                tab[RE16, :, cols], tab[IM16, :, cols] = re, im
            elif power == 2 * steps:
                tab[RE32, :, cols], tab[IM32, :, cols] = re, im
            elif power == 4 * steps:
                tab[RE64, :, cols], tab[IM64, :, cols] = re, im
            elif power == 8 * steps:
                tab[RE128, :, cols], tab[IM128, :, cols] = re, im
        return carry

    lax.fori_loop(0, blocks, parameters, 0)
    if 4 * per_owner < msg_rows:
        t_send[...] = jnp.zeros(t_send.shape, F32)
        rot_a[...] = jnp.zeros(rot_a.shape, F32)
        rot_b[...] = jnp.zeros(rot_b.shape, F32)
    own = lax.rem(me, owners)
    for pole in range(2):
        for k in range(per_owner):
            cols = pl.ds(pl.multiple_of((own * per_owner + k) * LANES, LANES), LANES)
            re, im = tab[RE128, pole : pole + 1, cols], tab[IM128, pole : pole + 1, cols]
            row = pole * per_owner + k
            rot_a[row : row + 1, :] = re
            rot_a[half_msg + row : half_msg + row + 1, :] = re
            rot_b[row : row + 1, :] = -im
            rot_b[half_msg + row : half_msg + row + 1, :] = im

    pl.when(me > 0)(halo_copy.wait_recv)
    keep = me > 0
    received = halo_recv[...].astype(F32)
    received = jnp.where(keep, received, jnp.zeros_like(received))
    halo[:, 0:half_width] = received[0:8]
    halo[:, half_width:width] = received[8:16]

    sub = lax.broadcasted_iota(jnp.int32, (CHUNKS, WIDE), 0)
    first = sub == 0

    def param(which, pole, cols):
        return tab[which, pole : pole + 1, cols]

    def short(i, cols):
        x = jnp.dot(to_chunks[...], xs[i, :, cols], preferred_element_type=F32)
        at = [x[CHUNKS * r : CHUNKS * (r + 1)] for r in range(steps)]
        before2 = jnp.where(first, halo[2 * i : 2 * i + 1, cols], pltpu.roll(at[steps - 2], 1, 0))
        before1 = jnp.where(first, halo[2 * i + 1 : 2 * i + 2, cols], pltpu.roll(at[steps - 1], 1, 0))
        at = [before2, before1] + at
        w = [taps[tap, i : i + 1, cols] for tap in range(3)]
        return [w[0] * at[r] + w[1] * at[r + 1] + w[2] * at[r + 2] for r in range(steps)]

    def message_place(b, k):
        if per_owner == 1:
            return (WIDE // LANES) * b + k, 0
        tile = (WIDE // LANES) * b + k
        return tile // per_owner, tile % per_owner

    def pass_a(b, carry):
        cols = pl.ds(pl.multiple_of(b * WIDE, WIDE), WIDE)
        key = short(1, cols)
        value = short(2, cols)
        c1 = [param(C1, pole, cols) for pole in range(2)]
        c2 = [param(C2, pole, cols) for pole in range(2)]
        now = [jnp.zeros((CHUNKS, WIDE), F32)] * 2
        old = [jnp.zeros((CHUNKS, WIDE), F32)] * 2
        for r in range(steps):
            p = key[r] * value[r]
            prod[CHUNKS * r : CHUNKS * (r + 1), cols] = p
            for pole in range(2):
                now[pole], old[pole] = p + c1[pole] * now[pole] + c2[pole] * old[pole], now[pole]
        for pole in range(2):
            re = now[pole] - param(RE1, pole, cols) * old[pole]
            im = param(IM1, pole, cols) * old[pole]
            for shift, wr, wi in ((1, RE16, IM16), (2, RE32, IM32), (4, RE64, IM64)):
                wr, wi = param(wr, pole, cols), param(wi, pole, cols)
                far = sub >= shift
                pr = jnp.where(far, pltpu.roll(re, shift, 0), 0.0)
                pi = jnp.where(far, pltpu.roll(im, shift, 0), 0.0)
                re, im = re + (wr * pr - wi * pi), im + (wr * pi + wi * pr)
            scan[2 * pole, :, cols] = jnp.where(first, 0.0, pltpu.roll(re, 1, 0))
            scan[2 * pole + 1, :, cols] = jnp.where(first, 0.0, pltpu.roll(im, 1, 0))
            for k in range(WIDE // LANES):
                owner, kk = message_place(b, k)
                lanes = slice(k * LANES, (k + 1) * LANES)
                row = pole * per_owner + kk
                t_send[owner, pl.ds(row, 1), :] = re[CHUNKS - 1 : CHUNKS, lanes]
                t_send[owner, pl.ds(half_msg + row, 1), :] = im[CHUNKS - 1 : CHUNKS, lanes]
        return carry

    def part_a(part, carry):
        kv_copy(part).wait()
        each = part_width // WIDE
        return lax.fori_loop(part * each, (part + 1) * each, pass_a, carry)

    lax.fori_loop(0, kv_parts, part_a, 0)

    def t_copy(source, target):
        return pltpu.make_async_remote_copy(
            src_ref=t_send.at[target],
            dst_ref=t_in.at[source],
            send_sem=t_ssem.at[target],
            recv_sem=t_rsem.at[source],
            device_id={"seq": target},
            device_id_type=MESH,
        )

    def c_copy(source, target):
        return pltpu.make_async_remote_copy(
            src_ref=c_out.at[target],
            dst_ref=c_in.at[source],
            send_sem=c_ssem.at[target],
            recv_sem=c_rsem.at[source],
            device_id={"seq": target},
            device_id_type=MESH,
        )

    def when_owner(device, action):
        if owners == n:
            action()
        else:
            pl.when(device < owners)(action)

    def send_t(d, carry):
        target = lax.rem(me + d, n)
        when_owner(target, lambda: t_copy(me, target).start())
        return carry

    lax.fori_loop(1, n, send_t, 0)

    q_copy.wait()

    def pass_b(b, carry):
        cols = pl.ds(pl.multiple_of(b * WIDE, WIDE), WIDE)
        for r, values in enumerate(short(0, cols)):
            query[CHUNKS * r : CHUNKS * (r + 1), cols] = values
        return carry

    def pass_b2(b, carry):
        cols = pl.ds(pl.multiple_of(b * WIDE, WIDE), WIDE)
        c1 = [param(C1, pole, cols) for pole in range(2)]
        c2 = [param(C2, pole, cols) for pole in range(2)]
        g0 = [param(G0, pole, cols) for pole in range(2)]
        g1 = [param(G1, pole, cols) for pole in range(2)]
        gain = skip[:, cols]
        zero = jnp.zeros((CHUNKS, WIDE), F32)
        now, old, before = [zero] * 2, [zero] * 2, zero
        for r in range(steps):
            p = prod[CHUNKS * r : CHUNKS * (r + 1), cols]
            for pole in range(2):
                fresh = g0[pole] * p + g1[pole] * before + c1[pole] * now[pole] + c2[pole] * old[pole]
                now[pole], old[pole] = fresh, now[pole]
            local[CHUNKS * r : CHUNKS * (r + 1), cols] = now[0] + now[1] + gain * p
            before = p
        return carry

    lax.fori_loop(0, blocks, pass_b, 0)

    def owner_step():
        t_in[pl.ds(me, 1)] = t_send[pl.ds(own, 1)]

        def wait_t(d, carry):
            t_copy(lax.rem(me + d, n), me).wait_recv()
            return carry

        lax.fori_loop(1, n, wait_t, 0)
        a, bb = rot_a[...], rot_b[...]

        def prefix(i, state):
            c_out[i] = state
            return a * state + bb * pltpu.roll(state, half_msg, 0) + t_in[i]

        lax.fori_loop(0, n, prefix, jnp.zeros((msg_rows, LANES), F32))

        def send_c(d, carry):
            c_copy(me, lax.rem(me + d, n)).start()
            return carry

        lax.fori_loop(1, n, send_c, 0)
        c_in[pl.ds(own, 1)] = c_out[pl.ds(me, 1)]

    when_owner(me, owner_step)

    lax.fori_loop(0, blocks, pass_b2, 0)

    def wait_c(d, carry):
        source = lax.rem(me + d, n)
        when_owner(source, lambda: c_copy(source, me).wait_recv())
        return carry

    lax.fori_loop(1, n, wait_c, 0)

    def out_copy(b):
        cols = pl.ds(pl.multiple_of(b * WIDE, WIDE), WIDE)
        return pltpu.make_async_copy(outs.at[:, cols], out_hbm.at[:, cols], out_sems.at[b])

    def pass_c(b, carry):
        cols = pl.ds(pl.multiple_of(b * WIDE, WIDE), WIDE)
        c1 = [param(C1, pole, cols) for pole in range(2)]
        c2 = [param(C2, pole, cols) for pole in range(2)]
        now, old = [], []
        for pole in range(2):
            cr, ci = [], []
            for k in range(WIDE // LANES):
                owner, kk = message_place(b, k)
                row = pole * per_owner + kk
                cr.append(c_in[owner, pl.ds(row, 1), :])
                ci.append(c_in[owner, pl.ds(half_msg + row, 1), :])
            cr = jnp.broadcast_to(jnp.concatenate(cr, axis=1), (CHUNKS, WIDE))
            ci = jnp.broadcast_to(jnp.concatenate(ci, axis=1), (CHUNKS, WIDE))
            for bit, wr, wi in ((1, RE16, IM16), (2, RE32, IM32), (4, RE64, IM64)):
                wr, wi = param(wr, pole, cols), param(wi, pole, cols)
                has = (sub // bit) % 2 == 1
                cr, ci = (
                    jnp.where(has, wr * cr - wi * ci, cr),
                    jnp.where(has, wr * ci + wi * cr, ci),
                )
            zr = scan[2 * pole, :, cols] + cr
            zi = scan[2 * pole + 1, :, cols] + ci
            old.append(param(G0, pole, cols) * zr + param(H1, pole, cols) * zi)
            now.append(param(H0R, pole, cols) * zr + param(H0I, pole, cols) * zi)
        done = []
        for r in range(steps):
            at = slice(CHUNKS * r, CHUNKS * (r + 1))
            done.append(query[at, cols] * (local[at, cols] + (now[0] + now[1])))
            for pole in range(2):
                now[pole], old[pole] = c1[pole] * now[pole] + c2[pole] * old[pole], now[pole]
        gated = jnp.concatenate(done, axis=0).astype(BF16)
        outs[:, cols] = jnp.dot(to_rows[...], gated, preferred_element_type=F32).astype(BF16)
        out_copy(b).start()
        return carry

    lax.fori_loop(0, blocks, pass_c, 0)

    def wait_out(b, carry):
        out_copy(b).wait()
        return carry

    lax.fori_loop(0, blocks, wait_out, 0)

    def drain(d, carry):
        target = lax.rem(me + d, n)
        when_owner(target, lambda: t_copy(me, target).wait_send())
        when_owner(me, lambda: c_copy(me, target).wait_send())
        return carry

    lax.fori_loop(1, n, drain, 0)
    pl.when(me < n - 1)(halo_copy.wait_send)


def solution(mesh):
    n = mesh.shape["seq"]

    def on_device(projected, short_taps, skip_gain, residues, pole_angles, decay_rates):
        _, rows, width = projected.shape
        tiles = width // LANES
        owners = min(n, tiles)
        per_owner = tiles // owners
        msg_rows = max(8, 4 * per_owner)
        kv_parts = 4
        dma = pltpu.SemaphoreType.DMA
        vmem = pltpu.VMEM
        return pl.pallas_call(
            functools.partial(kernel, n, owners, per_owner),
            out_shape=jax.ShapeDtypeStruct((rows, width), BF16),
            in_specs=[pl.BlockSpec(memory_space=pl.ANY)] * 6,
            out_specs=pl.BlockSpec(memory_space=pl.ANY),
            scratch_shapes=[
                vmem((3, rows, width), BF16),
                vmem((3, 16, width), BF16),
                vmem(short_taps.shape, F32),
                vmem((1, width), F32),
                vmem(residues.shape, F32),
                vmem(pole_angles.shape, F32),
                vmem(decay_rates.shape, F32),
                vmem((rows, rows), BF16),
                vmem((rows, rows), BF16),
                vmem((TABLE_ROWS, 2, width), F32),
                vmem((16, width // 2), F32),
                vmem((16, width // 2), BF16),
                vmem((16, width // 2), BF16),
                vmem((8, width), F32),
                vmem((rows, width), F32),
                vmem((rows, width), F32),
                vmem((rows, width), F32),
                vmem((4, CHUNKS, width), F32),
                vmem((owners, msg_rows, LANES), F32),
                vmem((n, msg_rows, LANES), F32),
                vmem((n, msg_rows, LANES), F32),
                vmem((owners, msg_rows, LANES), F32),
                vmem((msg_rows, LANES), F32),
                vmem((msg_rows, LANES), F32),
                vmem((rows, width), BF16),
                dma((7,)),
                dma((kv_parts,)),
                dma((width // WIDE,)),
                dma((2,)),
                dma((n,)),
                dma((n,)),
                dma((n,)),
                dma((n,)),
            ],
            compiler_params=pltpu.CompilerParams(
                collective_id=0, has_side_effects=True, vmem_limit_bytes=40 * 1024 * 1024
            ),
            cost_estimate=pl.CostEstimate(
                flops=60 * rows * width, bytes_accessed=8 * rows * width, transcendentals=2 * width
            ),
        )(projected, short_taps, skip_gain.reshape(1, width), residues, pole_angles, decay_rates)

    return jax.shard_map(
        on_device,
        mesh=mesh,
        in_specs=(P(None, ("grp", "seq"), None), P(), P(), P(), P(), P()),
        out_specs=P(("grp", "seq"), None),
        check_vma=False,
    )
```

profile of v0, /device:TPU:0, one launch (start us, length us, event | category | flops | bytes accessed | tf_op | source)
XLA Modules:
  0.0 33.5 jit_solution(9159526760599337912)
XLA Ops:
  0.0 0.0 copy-start
  0.0 1.9 %copy-done = bf16[3,128,4096]{2,1,0:T(8,128)(2,1)S(1)} copy-done((bf16[3,128,4096]{2,1,0:T(8,128)(2,1)S(1)}, bf16[3,128,4096]{2,1,0:T(8,128)(2,1)}, u32[]{:S(2)}) %copy-start) | copy-done | bytes 3145752
  1.9 0.0 copy-start.1
  1.9 0.9 %copy-done.1 = f32[3,3,4096]{2,1,0:T(4,128)S(1)} copy-done((f32[3,3,4096]{2,1,0:T(4,128)S(1)}, f32[3,3,4096]{2,1,0:T(4,128)}, u32[]{:S(2)}) %copy-start.1) | copy-done | bytes 147480
  2.8 0.0 copy-start.2
  2.8 0.8 %copy-done.2 = f32[2,2,4096]{2,1,0:T(2,128)S(1)} copy-done((f32[2,2,4096]{2,1,0:T(2,128)S(1)}, f32[2,2,4096]{2,1,0:T(2,128)}, u32[]{:S(2)}) %copy-start.2) | copy-done | bytes 65560
  3.7 0.0 copy-start.3
  3.7 0.8 %copy-done.3 = f32[2,4096]{1,0:T(2,128)S(1)} copy-done((f32[2,4096]{1,0:T(2,128)S(1)}, f32[2,4096]{1,0:T(2,128)}, u32[]{:S(2)}) %copy-start.3) | copy-done | bytes 32792
  4.4 0.0 copy-start.4
  4.4 0.8 %copy-done.4 = f32[2,4096]{1,0:T(2,128)S(1)} copy-done((f32[2,4096]{1,0:T(2,128)S(1)}, f32[2,4096]{1,0:T(2,128)}, u32[]{:S(2)}) %copy-start.4) | copy-done | bytes 32792
  5.2 0.0 copy-start.5
  5.2 0.7 %copy-done.5 = f32[4096]{0:T(1024)S(1)} copy-done((f32[4096]{0:T(1024)S(1)}, f32[4096]{0:T(1024)}, u32[]{:S(2)}) %copy-start.5) | copy-done | bytes 16408
  5.9 26.6 %shard_map.64 = bf16[128,4096]{1,0:T(8,128)(2,1)S(1)} custom-call(bf16[3,128,4096]{2,1,0:T(8,128)(2,1)S(1)} %copy-done, f32[3,3,4096]{2,1,0:T(4,128)S(1)} %copy-done.1, f32[1,4096]{1,0:T(1,128)S(1)} %bitcast.1, f32[2,2,4096]{2,1,0:T(2,128)S(1)} %copy-done.2, f32[2,4096]{1,0:T(2,128)S(1)} %copy-done.3, f32[2,4096]{1,0:T(2,128)S(1)} %copy-done.4), custom_call_target="tpu_custom_call" | custom-call | flops 31457280 | bytes 4194304 | tf_op jit(solution)/shard_map/pallas_call | solution.py:391
  32.5 1.0 %copy.8 = bf16[128,4096]{1,0:T(8,128)(2,1)} copy(bf16[128,4096]{1,0:T(8,128)(2,1)S(1)} %shard_map.64) | data formatting | bytes 2097152
Async XLA Ops:
  0.0 1.9 %copy-start = (bf16[3,128,4096]{2,1,0:T(8,128)(2,1)S(1)}, bf16[3,128,4096]{2,1,0:T(8,128)(2,1)}, u32[]{:S(2)}) copy-start(bf16[3,128,4096]{2,1,0:T(8,128)(2,1)} %x_hbm.1) | copy-start | bytes 9437188
  1.9 0.9 %copy-start.1 = (f32[3,3,4096]{2,1,0:T(4,128)S(1)}, f32[3,3,4096]{2,1,0:T(4,128)}, u32[]{:S(2)}) copy-start(f32[3,3,4096]{2,1,0:T(4,128)} %taps_hbm.1) | copy-start | bytes 442372
  2.8 0.8 %copy-start.2 = (f32[2,2,4096]{2,1,0:T(2,128)S(1)}, f32[2,2,4096]{2,1,0:T(2,128)}, u32[]{:S(2)}) copy-start(f32[2,2,4096]{2,1,0:T(2,128)} %res_hbm.1) | copy-start | bytes 196612
  3.7 0.8 %copy-start.3 = (f32[2,4096]{1,0:T(2,128)S(1)}, f32[2,4096]{1,0:T(2,128)}, u32[]{:S(2)}) copy-start(f32[2,4096]{1,0:T(2,128)} %ang_hbm.1) | copy-start | bytes 98308
  4.4 0.8 %copy-start.4 = (f32[2,4096]{1,0:T(2,128)S(1)}, f32[2,4096]{1,0:T(2,128)}, u32[]{:S(2)}) copy-start(f32[2,4096]{1,0:T(2,128)} %dec_hbm.1) | copy-start | bytes 98308
  5.2 0.7 %copy-start.5 = (f32[4096]{0:T(1024)S(1)}, f32[4096]{0:T(1024)}, u32[]{:S(2)}) copy-start(f32[4096]{0:T(1024)} %param.8) | copy-start | bytes 49156
where the time goes:
time: 33.9 us; the launch traced here: 33.5 us
  Pallas kernels  26.6 us (78%)
  local copies, waits for them, and re-layouts  6.86 us (20%)
    pallas_call x1, Pallas kernels, on_device(): pl.pallas_call(functools.partial(kernel, n, owners, per_owner), out_shape...  26.6 us
    unnamed x13, local copies, waits for them, and re-layouts  6.86 us

commit v1 on v0

--- a/solution.py
+++ b/solution.py
@@ -10,7 +10,7 @@
 MESH = pl.DeviceIdType.MESH
 LANES = 128
 CHUNKS = 8
-WIDE = 256
+WIDE = 512
 F32 = jnp.float32
 BF16 = jnp.bfloat16
 
@@ -37,7 +37,7 @@
 def kernel(
     n, owners, per_owner,
     x_hbm, taps_hbm, skip_hbm, res_hbm, ang_hbm, dec_hbm, out_hbm,
-    xs, tail, taps, skip, res, ang, dec, to_chunks, to_rows, tab,
+    xs, ordered, tail, taps, skip, res, ang, dec, to_chunks, to_rows, tab,
     halo_f32, halo_send, halo_recv, halo,
     prod, local, query, scan, t_send, t_in, c_out, c_in, rot_a, rot_b, outs,
     in_sems, kv_sems, out_sems, halo_sems, t_ssem, t_rsem, c_ssem, c_rsem,
@@ -105,14 +105,11 @@
         device_id={"seq": lax.rem(me + 1, n)},
         device_id_type=MESH,
     )
-    pl.semaphore_wait(barrier, n - 1)
-    pl.when(me < n - 1)(halo_copy.start)
-
     for copy in small:
         copy.wait()
 
     def parameters(b, carry):
-        cols = pl.ds(pl.multiple_of(b * WIDE, WIDE), WIDE)
+        cols = pl.ds(pl.multiple_of(b * part_width, part_width), part_width)
         c, s = cos_sin_half(ang[:, cols])
         root = jnp.exp(-0.5 * dec[:, cols])
         re, im = square(root * c, root * s)
@@ -140,7 +137,22 @@
                 tab[RE128, :, cols], tab[IM128, :, cols] = re, im
         return carry
 
-    lax.fori_loop(0, blocks, parameters, 0)
+    lax.fori_loop(0, kv_parts, parameters, 0)
+    pl.semaphore_wait(barrier, n - 1)
+    pl.when(me < n - 1)(halo_copy.start)
+
+    def order(i, part):
+        cols = pl.ds(pl.multiple_of(part * part_width, part_width), part_width)
+        ordered[i, :, cols] = jnp.dot(to_chunks[...], xs[i, :, cols], preferred_element_type=F32)
+
+    def order_kv(part, carry):
+        kv_copy(part).wait()
+        order(1, part)
+        order(2, part)
+        return carry
+
+    lax.fori_loop(0, kv_parts, order_kv, 0)
+
     if 4 * per_owner < msg_rows:
         t_send[...] = jnp.zeros(t_send.shape, F32)
         rot_a[...] = jnp.zeros(rot_a.shape, F32)
@@ -170,8 +182,7 @@
         return tab[which, pole : pole + 1, cols]
 
     def short(i, cols):
-        x = jnp.dot(to_chunks[...], xs[i, :, cols], preferred_element_type=F32)
-        at = [x[CHUNKS * r : CHUNKS * (r + 1)] for r in range(steps)]
+        at = [ordered[i, CHUNKS * r : CHUNKS * (r + 1), cols] for r in range(steps)]
         before2 = jnp.where(first, halo[2 * i : 2 * i + 1, cols], pltpu.roll(at[steps - 2], 1, 0))
         before1 = jnp.where(first, halo[2 * i + 1 : 2 * i + 2, cols], pltpu.roll(at[steps - 1], 1, 0))
         at = [before2, before1] + at
@@ -216,12 +227,7 @@
                 t_send[owner, pl.ds(half_msg + row, 1), :] = im[CHUNKS - 1 : CHUNKS, lanes]
         return carry
 
-    def part_a(part, carry):
-        kv_copy(part).wait()
-        each = part_width // WIDE
-        return lax.fori_loop(part * each, (part + 1) * each, pass_a, carry)
-
-    lax.fori_loop(0, kv_parts, part_a, 0)
+    lax.fori_loop(0, blocks, pass_a, 0)
 
     def t_copy(source, target):
         return pltpu.make_async_remote_copy(
@@ -257,6 +263,12 @@
     lax.fori_loop(1, n, send_t, 0)
 
     q_copy.wait()
+
+    def order_q(part, carry):
+        order(0, part)
+        return carry
+
+    lax.fori_loop(0, kv_parts, order_q, 0)
 
     def pass_b(b, carry):
         cols = pl.ds(pl.multiple_of(b * WIDE, WIDE), WIDE)
@@ -395,6 +407,7 @@
             out_specs=pl.BlockSpec(memory_space=pl.ANY),
             scratch_shapes=[
                 vmem((3, rows, width), BF16),
+                vmem((3, rows, width), F32),
                 vmem((3, 16, width), BF16),
                 vmem(short_taps.shape, F32),
                 vmem((1, width), F32),
@@ -429,7 +442,7 @@
                 dma((n,)),
             ],
             compiler_params=pltpu.CompilerParams(
-                collective_id=0, has_side_effects=True, vmem_limit_bytes=40 * 1024 * 1024
+                collective_id=0, has_side_effects=True, vmem_limit_bytes=63 * 1024 * 1024
             ),
             cost_estimate=pl.CostEstimate(
                 flops=60 * rows * width, bytes_accessed=8 * rows * width, transcendentals=2 * width

time: 33.9 us -> 25.1 us (0.74)
  local copies, waits for them, and re-layouts: 6.86 us -> 2.29 us
  Pallas kernels: 26.6 us -> 22.7 us
    unnamed x13 -> x1, local copies, waits for them, and re-layouts: 6.86 us -> 2.29 us
    pallas_call x1, Pallas kernels: 26.6 us -> 22.7 us  [on_device(): pl.pallas_call(functools.partial(kernel, n, owners, per_owner), out_shape...]
where the time goes in v1:
time: 25.1 us; the launch traced here: 25 us
  Pallas kernels  22.7 us (90%)
  local copies, waits for them, and re-layouts  2.29 us (9%)
    pallas_call x1, Pallas kernels, on_device(): pl.pallas_call(functools.partial(kernel, n, owners, per_owner), out_shape...  22.7 us
    unnamed x1, local copies, waits for them, and re-layouts  2.29 us

profile of v1, /device:TPU:0, one launch (start us, length us, event | category | flops | bytes accessed | tf_op | source)
XLA Modules:
  0.0 25.0 jit_solution(6440986042739530729)
XLA Ops:
  0.0 22.7 %shard_map.64 = bf16[128,4096]{1,0:T(8,128)(2,1)} custom-call(bf16[3,128,4096]{2,1,0:T(8,128)(2,1)} %x_hbm.1, f32[3,3,4096]{2,1,0:T(4,128)} %taps_hbm.1, f32[1,4096]{1,0:T(1,128)} %bitcast.1, f32[2,2,4096]{2,1,0:T(2,128)} %res_hbm.1, f32[2,4096]{1,0:T(2,128)} %ang_hbm.1, f32[2,4096]{1,0:T(2,128)} %dec_hbm.1), custom_call_target="tpu_custom_call" | custom-call | flops 31457280 | bytes 4194304 | tf_op jit(solution)/shard_map/pallas_call | solution.py:403
  22.7 2.3 %copy.8 = bf16[128,4096]{1,0:T(8,128)(2,1)} copy(bf16[128,4096]{1,0:T(8,128)(2,1)} %shard_map.64) | data formatting | bytes 2097152

commit v2 on v1

--- a/solution.py
+++ b/solution.py
@@ -1,4 +1,5 @@
 import functools
+import math
 
 import jax
 import jax.numpy as jnp
@@ -8,9 +9,8 @@
 from jax.sharding import PartitionSpec as P
 
 MESH = pl.DeviceIdType.MESH
-LANES = 128
 CHUNKS = 8
-WIDE = 512
+WIDE = 256
 F32 = jnp.float32
 BF16 = jnp.bfloat16
 
@@ -35,12 +35,12 @@
 
 
 def kernel(
-    n, owners, per_owner,
+    n, members,
     x_hbm, taps_hbm, skip_hbm, res_hbm, ang_hbm, dec_hbm, out_hbm,
     xs, ordered, tail, taps, skip, res, ang, dec, to_chunks, to_rows, tab,
     halo_f32, halo_send, halo_recv, halo,
-    prod, local, query, scan, t_send, t_in, c_out, c_in, rot_a, rot_b, outs,
-    in_sems, kv_sems, out_sems, halo_sems, t_ssem, t_rsem, c_ssem, c_rsem,
+    prod, local, query, scan, t_send, t_in, c_out, c_in, chain_out, chain_in, outs,
+    in_sems, kv_sems, out_sems, halo_sems, t_ssem, t_rsem, c_ssem, c_rsem, chain_sems, ready,
 ):
     rows, width = xs.shape[1], xs.shape[2]
     steps = rows // CHUNKS
@@ -48,17 +48,34 @@
     blocks = width // WIDE
     kv_parts = kv_sems.shape[0]
     part_width = width // kv_parts
-    msg_rows = t_send.shape[1]
-    half_msg = msg_rows // 2
+    quarter = width // members
     me = lax.axis_index("seq")
+    place = lax.rem(me, members)
+    base = me - place
+    has_group_before = base > 0
+    has_group_after = base + members < n
+    is_first = place == 0
+    is_last = place == members - 1
+
+    def peer(step):
+        other = place + step
+        return jnp.where(other >= members, other - members, other)
 
     barrier = pltpu.get_barrier_semaphore()
 
-    def greet(d, carry):
-        pl.semaphore_signal(
-            barrier, inc=1, device_id={"seq": lax.rem(me + d, n)}, device_id_type=MESH
-        )
-        return carry
+    def signal(semaphore, device):
+        pl.semaphore_signal(semaphore, inc=1, device_id={"seq": device}, device_id_type=MESH)
+
+    for step in range(1, members):
+        signal(barrier, base + peer(step))
+
+    @pl.when(has_group_after)
+    def _():
+        signal(barrier, me + members)
+
+    @pl.when(has_group_after & is_last)
+    def _():
+        signal(barrier, me + 1)
 
     def kv_copy(part):
         cols = pl.ds(pl.multiple_of(part * part_width, part_width), part_width)
@@ -82,12 +99,11 @@
         kv_copy(part).start()
     q_copy = pltpu.make_async_copy(x_hbm.at[0], xs.at[0], in_sems.at[6])
     q_copy.start()
-    lax.fori_loop(1, n, greet, 0)
 
     i0 = lax.broadcasted_iota(jnp.int32, (rows, rows), 0)
     i1 = lax.broadcasted_iota(jnp.int32, (rows, rows), 1)
-    to_chunks[...] = jnp.where(i1 == (i0 % CHUNKS) * steps + i0 // CHUNKS, 1.0, 0.0).astype(BF16)
-    to_rows[...] = jnp.where(i0 == (i1 % CHUNKS) * steps + i1 // CHUNKS, 1.0, 0.0).astype(BF16)
+    to_chunks[...] = jnp.where(i1 == (i0 & (CHUNKS - 1)) * steps + (i0 >> 3), 1.0, 0.0).astype(BF16)
+    to_rows[...] = jnp.where(i0 == (i1 & (CHUNKS - 1)) * steps + (i1 >> 3), 1.0, 0.0).astype(BF16)
 
     tail_copy.wait()
     for i in range(3):
@@ -102,7 +118,7 @@
         dst_ref=halo_recv,
         send_sem=halo_sems.at[0],
         recv_sem=halo_sems.at[1],
-        device_id={"seq": lax.rem(me + 1, n)},
+        device_id={"seq": jnp.where(me < n - 1, me + 1, 0)},
         device_id_type=MESH,
     )
     for copy in small:
@@ -138,7 +154,21 @@
         return carry
 
     lax.fori_loop(0, kv_parts, parameters, 0)
-    pl.semaphore_wait(barrier, n - 1)
+    before = jnp.where(has_group_before, 1, 0)
+    pl.semaphore_wait(barrier, members - 1 + before + jnp.where(is_first, before, 0))
+
+    @pl.when(has_group_before)
+    def _():
+        signal(ready.at[0], me - members)
+
+    @pl.when(has_group_before & is_first)
+    def _():
+        signal(ready.at[1], me - 1)
+
+    @pl.when(has_group_after & is_last)
+    def _():
+        pl.semaphore_wait(ready.at[1], 1)
+
     pl.when(me < n - 1)(halo_copy.start)
 
     def order(i, part):
@@ -152,21 +182,6 @@
         return carry
 
     lax.fori_loop(0, kv_parts, order_kv, 0)
-
-    if 4 * per_owner < msg_rows:
-        t_send[...] = jnp.zeros(t_send.shape, F32)
-        rot_a[...] = jnp.zeros(rot_a.shape, F32)
-        rot_b[...] = jnp.zeros(rot_b.shape, F32)
-    own = lax.rem(me, owners)
-    for pole in range(2):
-        for k in range(per_owner):
-            cols = pl.ds(pl.multiple_of((own * per_owner + k) * LANES, LANES), LANES)
-            re, im = tab[RE128, pole : pole + 1, cols], tab[IM128, pole : pole + 1, cols]
-            row = pole * per_owner + k
-            rot_a[row : row + 1, :] = re
-            rot_a[half_msg + row : half_msg + row + 1, :] = re
-            rot_b[row : row + 1, :] = -im
-            rot_b[half_msg + row : half_msg + row + 1, :] = im
 
     pl.when(me > 0)(halo_copy.wait_recv)
     keep = me > 0
@@ -179,21 +194,20 @@
     first = sub == 0
 
     def param(which, pole, cols):
-        return tab[which, pole : pole + 1, cols]
+        return jnp.broadcast_to(tab[which, pole : pole + 1, cols], (CHUNKS, WIDE))
 
     def short(i, cols):
         at = [ordered[i, CHUNKS * r : CHUNKS * (r + 1), cols] for r in range(steps)]
         before2 = jnp.where(first, halo[2 * i : 2 * i + 1, cols], pltpu.roll(at[steps - 2], 1, 0))
         before1 = jnp.where(first, halo[2 * i + 1 : 2 * i + 2, cols], pltpu.roll(at[steps - 1], 1, 0))
         at = [before2, before1] + at
-        w = [taps[tap, i : i + 1, cols] for tap in range(3)]
+        w = [jnp.broadcast_to(taps[tap, i : i + 1, cols], (CHUNKS, WIDE)) for tap in range(3)]
         return [w[0] * at[r] + w[1] * at[r + 1] + w[2] * at[r + 2] for r in range(steps)]
 
-    def message_place(b, k):
-        if per_owner == 1:
-            return (WIDE // LANES) * b + k, 0
-        tile = (WIDE // LANES) * b + k
-        return tile // per_owner, tile % per_owner
+    def message_place(b):
+        each = quarter // WIDE
+        owner = b // each
+        return owner, pl.ds(pl.multiple_of((b - owner * each) * WIDE, WIDE), WIDE)
 
     def pass_a(b, carry):
         cols = pl.ds(pl.multiple_of(b * WIDE, WIDE), WIDE)
@@ -207,7 +221,7 @@
             p = key[r] * value[r]
             prod[CHUNKS * r : CHUNKS * (r + 1), cols] = p
             for pole in range(2):
-                now[pole], old[pole] = p + c1[pole] * now[pole] + c2[pole] * old[pole], now[pole]
+                now[pole], old[pole] = (p + c2[pole] * old[pole]) + c1[pole] * now[pole], now[pole]
         for pole in range(2):
             re = now[pole] - param(RE1, pole, cols) * old[pole]
             im = param(IM1, pole, cols) * old[pole]
@@ -219,15 +233,12 @@
                 re, im = re + (wr * pr - wi * pi), im + (wr * pi + wi * pr)
             scan[2 * pole, :, cols] = jnp.where(first, 0.0, pltpu.roll(re, 1, 0))
             scan[2 * pole + 1, :, cols] = jnp.where(first, 0.0, pltpu.roll(im, 1, 0))
-            for k in range(WIDE // LANES):
-                owner, kk = message_place(b, k)
-                lanes = slice(k * LANES, (k + 1) * LANES)
-                row = pole * per_owner + kk
-                t_send[owner, pl.ds(row, 1), :] = re[CHUNKS - 1 : CHUNKS, lanes]
-                t_send[owner, pl.ds(half_msg + row, 1), :] = im[CHUNKS - 1 : CHUNKS, lanes]
-        return carry
-
-    lax.fori_loop(0, blocks, pass_a, 0)
+            owner, there = message_place(b)
+            t_send[owner, 0, pl.ds(pole, 1), there] = re[CHUNKS - 1 : CHUNKS]
+            t_send[owner, 1, pl.ds(pole, 1), there] = im[CHUNKS - 1 : CHUNKS]
+        return carry
+
+    lax.fori_loop(0, blocks, pass_a, 0, unroll=2)
 
     def t_copy(source, target):
         return pltpu.make_async_remote_copy(
@@ -235,7 +246,7 @@
             dst_ref=t_in.at[source],
             send_sem=t_ssem.at[target],
             recv_sem=t_rsem.at[source],
-            device_id={"seq": target},
+            device_id={"seq": base + target},
             device_id_type=MESH,
         )
 
@@ -245,22 +256,20 @@
             dst_ref=c_in.at[source],
             send_sem=c_ssem.at[target],
             recv_sem=c_rsem.at[source],
-            device_id={"seq": target},
+            device_id={"seq": base + target},
             device_id_type=MESH,
         )
 
-    def when_owner(device, action):
-        if owners == n:
-            action()
-        else:
-            pl.when(device < owners)(action)
-
-    def send_t(d, carry):
-        target = lax.rem(me + d, n)
-        when_owner(target, lambda: t_copy(me, target).start())
-        return carry
-
-    lax.fori_loop(1, n, send_t, 0)
+    chain_copy = pltpu.make_async_remote_copy(
+        src_ref=chain_out,
+        dst_ref=chain_in,
+        send_sem=chain_sems.at[0],
+        recv_sem=chain_sems.at[1],
+        device_id={"seq": jnp.where(has_group_after, me + members, me - base)},
+        device_id_type=MESH,
+    )
+    for step in range(1, members):
+        t_copy(place, peer(step)).start()
 
     q_copy.wait()
 
@@ -282,53 +291,58 @@
         c2 = [param(C2, pole, cols) for pole in range(2)]
         g0 = [param(G0, pole, cols) for pole in range(2)]
         g1 = [param(G1, pole, cols) for pole in range(2)]
-        gain = skip[:, cols]
+        gain = jnp.broadcast_to(skip[:, cols], (CHUNKS, WIDE))
         zero = jnp.zeros((CHUNKS, WIDE), F32)
         now, old, before = [zero] * 2, [zero] * 2, zero
         for r in range(steps):
             p = prod[CHUNKS * r : CHUNKS * (r + 1), cols]
             for pole in range(2):
-                fresh = g0[pole] * p + g1[pole] * before + c1[pole] * now[pole] + c2[pole] * old[pole]
+                fresh = ((g0[pole] * p + g1[pole] * before) + c2[pole] * old[pole]) + c1[pole] * now[pole]
                 now[pole], old[pole] = fresh, now[pole]
             local[CHUNKS * r : CHUNKS * (r + 1), cols] = now[0] + now[1] + gain * p
             before = p
         return carry
 
-    lax.fori_loop(0, blocks, pass_b, 0)
-
-    def owner_step():
-        t_in[pl.ds(me, 1)] = t_send[pl.ds(own, 1)]
-
-        def wait_t(d, carry):
-            t_copy(lax.rem(me + d, n), me).wait_recv()
-            return carry
-
-        lax.fori_loop(1, n, wait_t, 0)
-        a, bb = rot_a[...], rot_b[...]
-
-        def prefix(i, state):
-            c_out[i] = state
-            return a * state + bb * pltpu.roll(state, half_msg, 0) + t_in[i]
-
-        lax.fori_loop(0, n, prefix, jnp.zeros((msg_rows, LANES), F32))
-
-        def send_c(d, carry):
-            c_copy(me, lax.rem(me + d, n)).start()
-            return carry
-
-        lax.fori_loop(1, n, send_c, 0)
-        c_in[pl.ds(own, 1)] = c_out[pl.ds(me, 1)]
-
-    when_owner(me, owner_step)
-
-    lax.fori_loop(0, blocks, pass_b2, 0)
-
-    def wait_c(d, carry):
-        source = lax.rem(me + d, n)
-        when_owner(source, lambda: c_copy(source, me).wait_recv())
-        return carry
-
-    lax.fori_loop(1, n, wait_c, 0)
+    lax.fori_loop(0, blocks, pass_b, 0, unroll=2)
+
+    t_in[pl.ds(place, 1)] = t_send[pl.ds(place, 1)]
+    for step in range(1, members):
+        t_copy(peer(step), place).wait_recv()
+
+    @pl.when(has_group_before)
+    def _():
+        chain_copy.wait_recv()
+
+    @pl.when(jnp.logical_not(has_group_before))
+    def _():
+        chain_in[...] = jnp.zeros(chain_in.shape, F32)
+
+    mine = pl.ds(pl.multiple_of(place * quarter, quarter), quarter)
+    wr, wi = tab[RE128, :, mine], tab[IM128, :, mine]
+    re, im = chain_in[0], chain_in[1]
+    for member in range(members):
+        c_out[member, 0] = re
+        c_out[member, 1] = im
+        re, im = (
+            wr * re - wi * im + t_in[member, 0],
+            wr * im + wi * re + t_in[member, 1],
+        )
+    chain_out[0] = re
+    chain_out[1] = im
+
+    @pl.when(has_group_after)
+    def _():
+        pl.semaphore_wait(ready.at[0], 1)
+        chain_copy.start()
+
+    for step in range(1, members):
+        c_copy(place, peer(step)).start()
+    c_in[pl.ds(place, 1)] = c_out[pl.ds(place, 1)]
+
+    lax.fori_loop(0, blocks, pass_b2, 0, unroll=2)
+
+    for step in range(1, members):
+        c_copy(peer(step), place).wait_recv()
 
     def out_copy(b):
         cols = pl.ds(pl.multiple_of(b * WIDE, WIDE), WIDE)
@@ -340,17 +354,12 @@
         c2 = [param(C2, pole, cols) for pole in range(2)]
         now, old = [], []
         for pole in range(2):
-            cr, ci = [], []
-            for k in range(WIDE // LANES):
-                owner, kk = message_place(b, k)
-                row = pole * per_owner + kk
-                cr.append(c_in[owner, pl.ds(row, 1), :])
-                ci.append(c_in[owner, pl.ds(half_msg + row, 1), :])
-            cr = jnp.broadcast_to(jnp.concatenate(cr, axis=1), (CHUNKS, WIDE))
-            ci = jnp.broadcast_to(jnp.concatenate(ci, axis=1), (CHUNKS, WIDE))
+            owner, there = message_place(b)
+            cr = jnp.broadcast_to(c_in[owner, 0, pl.ds(pole, 1), there], (CHUNKS, WIDE))
+            ci = jnp.broadcast_to(c_in[owner, 1, pl.ds(pole, 1), there], (CHUNKS, WIDE))
             for bit, wr, wi in ((1, RE16, IM16), (2, RE32, IM32), (4, RE64, IM64)):
                 wr, wi = param(wr, pole, cols), param(wi, pole, cols)
-                has = (sub // bit) % 2 == 1
+                has = (sub & bit) > 0
                 cr, ci = (
                     jnp.where(has, wr * cr - wi * ci, cr),
                     jnp.where(has, wr * ci + wi * cr, ci),
@@ -364,13 +373,13 @@
             at = slice(CHUNKS * r, CHUNKS * (r + 1))
             done.append(query[at, cols] * (local[at, cols] + (now[0] + now[1])))
             for pole in range(2):
-                now[pole], old[pole] = c1[pole] * now[pole] + c2[pole] * old[pole], now[pole]
+                now[pole], old[pole] = c2[pole] * old[pole] + c1[pole] * now[pole], now[pole]
         gated = jnp.concatenate(done, axis=0).astype(BF16)
         outs[:, cols] = jnp.dot(to_rows[...], gated, preferred_element_type=F32).astype(BF16)
         out_copy(b).start()
         return carry
 
-    lax.fori_loop(0, blocks, pass_c, 0)
+    lax.fori_loop(0, blocks, pass_c, 0, unroll=2)
 
     def wait_out(b, carry):
         out_copy(b).wait()
@@ -378,13 +387,10 @@
 
     lax.fori_loop(0, blocks, wait_out, 0)
 
-    def drain(d, carry):
-        target = lax.rem(me + d, n)
-        when_owner(target, lambda: t_copy(me, target).wait_send())
-        when_owner(me, lambda: c_copy(me, target).wait_send())
-        return carry
-
-    lax.fori_loop(1, n, drain, 0)
+    for step in range(1, members):
+        t_copy(place, peer(step)).wait_send()
+        c_copy(place, peer(step)).wait_send()
+    pl.when(has_group_after)(chain_copy.wait_send)
     pl.when(me < n - 1)(halo_copy.wait_send)
 
 
@@ -393,15 +399,13 @@
 
     def on_device(projected, short_taps, skip_gain, residues, pole_angles, decay_rates):
         _, rows, width = projected.shape
-        tiles = width // LANES
-        owners = min(n, tiles)
-        per_owner = tiles // owners
-        msg_rows = max(8, 4 * per_owner)
+        members = math.gcd(n, 4)
+        quarter = width // members
         kv_parts = 4
         dma = pltpu.SemaphoreType.DMA
         vmem = pltpu.VMEM
         return pl.pallas_call(
-            functools.partial(kernel, n, owners, per_owner),
+            functools.partial(kernel, n, members),
             out_shape=jax.ShapeDtypeStruct((rows, width), BF16),
             in_specs=[pl.BlockSpec(memory_space=pl.ANY)] * 6,
             out_specs=pl.BlockSpec(memory_space=pl.ANY),
@@ -425,21 +429,23 @@
                 vmem((rows, width), F32),
                 vmem((rows, width), F32),
                 vmem((4, CHUNKS, width), F32),
-                vmem((owners, msg_rows, LANES), F32),
-                vmem((n, msg_rows, LANES), F32),
-                vmem((n, msg_rows, LANES), F32),
-                vmem((owners, msg_rows, LANES), F32),
-                vmem((msg_rows, LANES), F32),
-                vmem((msg_rows, LANES), F32),
+                vmem((members, 2, 2, quarter), F32),
+                vmem((members, 2, 2, quarter), F32),
+                vmem((members, 2, 2, quarter), F32),
+                vmem((members, 2, 2, quarter), F32),
+                vmem((2, 2, quarter), F32),
+                vmem((2, 2, quarter), F32),
                 vmem((rows, width), BF16),
                 dma((7,)),
                 dma((kv_parts,)),
                 dma((width // WIDE,)),
                 dma((2,)),
-                dma((n,)),
-                dma((n,)),
-                dma((n,)),
-                dma((n,)),
+                dma((members,)),
+                dma((members,)),
+                dma((members,)),
+                dma((members,)),
+                dma((2,)),
+                pltpu.SemaphoreType.REGULAR((2,)),
             ],
             compiler_params=pltpu.CompilerParams(
                 collective_id=0, has_side_effects=True, vmem_limit_bytes=63 * 1024 * 1024

time: 25.1 us -> 24.1 us (0.960)
  the two profiles are of different devices: /device:TPU:0 before, /device:TPU:25 now
where the time goes in v2:
time: 24.1 us; the launch traced here: 24 us
  Pallas kernels  21.7 us (90%)
  local copies, waits for them, and re-layouts  2.29 us (10%)
    pallas_call x1, Pallas kernels, on_device(): pl.pallas_call(functools.partial(kernel, n, members), out_shape=jax.Shape...  21.7 us
    unnamed x1, local copies, waits for them, and re-layouts  2.29 us

profile of v2, /device:TPU:25, one launch (start us, length us, event | category | flops | bytes accessed | tf_op | source)
XLA Modules:
  0.0 24.0 jit_solution(5428627777230664837)
XLA Ops:
  0.0 21.7 %shard_map.64 = bf16[128,4096]{1,0:T(8,128)(2,1)} custom-call(bf16[3,128,4096]{2,1,0:T(8,128)(2,1)} %x_hbm.1, f32[3,3,4096]{2,1,0:T(4,128)} %taps_hbm.1, f32[1,4096]{1,0:T(1,128)} %bitcast.1, f32[2,2,4096]{2,1,0:T(2,128)} %res_hbm.1, f32[2,4096]{1,0:T(2,128)} %ang_hbm.1, f32[2,4096]{1,0:T(2,128)} %dec_hbm.1), custom_call_target="tpu_custom_call" | custom-call | flops 31457280 | bytes 4194304 | tf_op jit(solution)/shard_map/pallas_call | solution.py:407
  21.7 2.3 %copy.8 = bf16[128,4096]{1,0:T(8,128)(2,1)} copy(bf16[128,4096]{1,0:T(8,128)(2,1)} %shard_map.64) | data formatting | bytes 2097152

commit v3 on v2

--- a/solution.py
+++ b/solution.py
@@ -39,8 +39,8 @@
     x_hbm, taps_hbm, skip_hbm, res_hbm, ang_hbm, dec_hbm, out_hbm,
     xs, ordered, tail, taps, skip, res, ang, dec, to_chunks, to_rows, tab,
     halo_f32, halo_send, halo_recv, halo,
-    prod, local, query, scan, t_send, t_in, c_out, c_in, chain_out, chain_in, outs,
-    in_sems, kv_sems, out_sems, halo_sems, t_ssem, t_rsem, c_ssem, c_rsem, chain_sems, ready,
+    prod, local, query, scan, t_send, t_in, c_out, c_in, g_out, g_in, outs,
+    in_sems, kv_sems, out_sems, halo_sems, t_ssem, t_rsem, c_ssem, c_rsem, g_ssem, g_rsem, ready, halo_ready,
 ):
     rows, width = xs.shape[1], xs.shape[2]
     steps = rows // CHUNKS
@@ -52,6 +52,8 @@
     me = lax.axis_index("seq")
     place = lax.rem(me, members)
     base = me - place
+    groups = n // members
+    group = base // members
     has_group_before = base > 0
     has_group_after = base + members < n
     is_first = place == 0
@@ -69,9 +71,11 @@
     for step in range(1, members):
         signal(barrier, base + peer(step))
 
-    @pl.when(has_group_after)
-    def _():
-        signal(barrier, me + members)
+    def in_later_groups(action):
+        for ahead in range(1, groups):
+            pl.when(group + ahead < groups)(functools.partial(action, ahead))
+
+    in_later_groups(lambda ahead: signal(barrier, me + ahead * members))
 
     @pl.when(has_group_after & is_last)
     def _():
@@ -154,20 +158,21 @@
         return carry
 
     lax.fori_loop(0, kv_parts, parameters, 0)
-    before = jnp.where(has_group_before, 1, 0)
-    pl.semaphore_wait(barrier, members - 1 + before + jnp.where(is_first, before, 0))
-
-    @pl.when(has_group_before)
-    def _():
-        signal(ready.at[0], me - members)
+    first_of_later = jnp.where(has_group_before & is_first, 1, 0)
+    pl.semaphore_wait(barrier, members - 1 + group + first_of_later)
+
+    for back in range(1, groups):
+        @pl.when(group >= back)
+        def _():
+            signal(ready.at[back], me - back * members)
 
     @pl.when(has_group_before & is_first)
     def _():
-        signal(ready.at[1], me - 1)
+        signal(halo_ready, me - 1)
 
     @pl.when(has_group_after & is_last)
     def _():
-        pl.semaphore_wait(ready.at[1], 1)
+        pl.semaphore_wait(halo_ready, 1)
 
     pl.when(me < n - 1)(halo_copy.start)
 
@@ -260,14 +265,16 @@
             device_id_type=MESH,
         )
 
-    chain_copy = pltpu.make_async_remote_copy(
-        src_ref=chain_out,
-        dst_ref=chain_in,
-        send_sem=chain_sems.at[0],
-        recv_sem=chain_sems.at[1],
-        device_id={"seq": jnp.where(has_group_after, me + members, me - base)},
-        device_id_type=MESH,
-    )
+    def g_copy(source, ahead):
+        return pltpu.make_async_remote_copy(
+            src_ref=g_out,
+            dst_ref=g_in.at[source],
+            send_sem=g_ssem.at[ahead],
+            recv_sem=g_rsem.at[source],
+            device_id={"seq": lax.rem(me + ahead * members, n)},
+            device_id_type=MESH,
+        )
+
     for step in range(1, members):
         t_copy(place, peer(step)).start()
 
@@ -309,31 +316,42 @@
     for step in range(1, members):
         t_copy(peer(step), place).wait_recv()
 
-    @pl.when(has_group_before)
-    def _():
-        chain_copy.wait_recv()
-
-    @pl.when(jnp.logical_not(has_group_before))
-    def _():
-        chain_in[...] = jnp.zeros(chain_in.shape, F32)
-
     mine = pl.ds(pl.multiple_of(place * quarter, quarter), quarter)
     wr, wi = tab[RE128, :, mine], tab[IM128, :, mine]
-    re, im = chain_in[0], chain_in[1]
+    re = im = jnp.zeros((2, quarter), F32)
+    inside = []
     for member in range(members):
-        c_out[member, 0] = re
-        c_out[member, 1] = im
+        inside.append((re, im))
         re, im = (
             wr * re - wi * im + t_in[member, 0],
             wr * im + wi * re + t_in[member, 1],
         )
-    chain_out[0] = re
-    chain_out[1] = im
-
-    @pl.when(has_group_after)
-    def _():
-        pl.semaphore_wait(ready.at[0], 1)
-        chain_copy.start()
+    g_out[0] = re
+    g_out[1] = im
+
+    def send_g(ahead):
+        pl.semaphore_wait(ready.at[ahead], 1)
+        g_copy(group, ahead).start()
+
+    in_later_groups(send_g)
+
+    gr, gi = wr, wi
+    span = 1
+    while span < members:
+        gr, gi = square(gr, gi)
+        span *= 2
+
+    def add_group(source, state):
+        re, im = state
+        g_copy(source, 1).wait_recv()
+        return gr * re - gi * im + g_in[source, 0], gr * im + gi * re + g_in[source, 1]
+
+    zero = jnp.zeros((2, quarter), F32)
+    re, im = lax.fori_loop(0, group, add_group, (zero, zero))
+    for member in range(members):
+        c_out[member, 0] = inside[member][0] + re
+        c_out[member, 1] = inside[member][1] + im
+        re, im = wr * re - wi * im, wr * im + wi * re
 
     for step in range(1, members):
         c_copy(place, peer(step)).start()
@@ -390,7 +408,7 @@
     for step in range(1, members):
         t_copy(place, peer(step)).wait_send()
         c_copy(place, peer(step)).wait_send()
-    pl.when(has_group_after)(chain_copy.wait_send)
+    in_later_groups(lambda ahead: g_copy(group, ahead).wait_send())
     pl.when(me < n - 1)(halo_copy.wait_send)
 
 
@@ -401,6 +419,7 @@
         _, rows, width = projected.shape
         members = math.gcd(n, 4)
         quarter = width // members
+        groups = n // members
         kv_parts = 4
         dma = pltpu.SemaphoreType.DMA
         vmem = pltpu.VMEM
@@ -434,7 +453,7 @@
                 vmem((members, 2, 2, quarter), F32),
                 vmem((members, 2, 2, quarter), F32),
                 vmem((2, 2, quarter), F32),
-                vmem((2, 2, quarter), F32),
+                vmem((groups, 2, 2, quarter), F32),
                 vmem((rows, width), BF16),
                 dma((7,)),
                 dma((kv_parts,)),
@@ -444,11 +463,13 @@
                 dma((members,)),
                 dma((members,)),
                 dma((members,)),
-                dma((2,)),
-                pltpu.SemaphoreType.REGULAR((2,)),
+                dma((groups,)),
+                dma((groups,)),
+                pltpu.SemaphoreType.REGULAR((groups,)),
+                pltpu.SemaphoreType.REGULAR,
             ],
             compiler_params=pltpu.CompilerParams(
-                collective_id=0, has_side_effects=True, vmem_limit_bytes=63 * 1024 * 1024
+                collective_id=0, has_side_effects=True, vmem_limit_bytes=52 * 1024 * 1024
             ),
             cost_estimate=pl.CostEstimate(
                 flops=60 * rows * width, bytes_accessed=8 * rows * width, transcendentals=2 * width

time: 24.1 us -> 25.8 us (1.071)
  local copies, waits for them, and re-layouts: 2.29 us -> 4.97 us
  Pallas kernels: 21.7 us -> 20.5 us
    unnamed x1 -> x11, local copies, waits for them, and re-layouts: 2.29 us -> 4.97 us
    pallas_call x1, Pallas kernels: 21.7 us -> 20.5 us  [on_device(): pl.pallas_call(functools.partial(kernel, n, members), out_shape=jax.Shape...]
where the time goes in v3:
time: 25.8 us; the launch traced here: 25.5 us
  Pallas kernels  20.5 us (79%)
  local copies, waits for them, and re-layouts  4.97 us (19%)
    pallas_call x1, Pallas kernels, on_device(): pl.pallas_call(functools.partial(kernel, n, members), out_shape=jax.Shape...  20.5 us
    unnamed x11, local copies, waits for them, and re-layouts  4.97 us

profile of v3, /device:TPU:25, one launch (start us, length us, event | category | flops | bytes accessed | tf_op | source)
XLA Modules:
  0.0 25.5 jit_solution(15430424873028527063)
XLA Ops:
  0.0 0.0 copy-start
  0.0 0.9 %copy-done = f32[3,3,4096]{2,1,0:T(4,128)S(1)} copy-done((f32[3,3,4096]{2,1,0:T(4,128)S(1)}, f32[3,3,4096]{2,1,0:T(4,128)}, u32[]{:S(2)}) %copy-start) | copy-done | bytes 147480
  0.9 0.0 copy-start.1
  0.9 0.8 %copy-done.1 = f32[2,2,4096]{2,1,0:T(2,128)S(1)} copy-done((f32[2,2,4096]{2,1,0:T(2,128)S(1)}, f32[2,2,4096]{2,1,0:T(2,128)}, u32[]{:S(2)}) %copy-start.1) | copy-done | bytes 65560
  1.8 0.0 copy-start.2
  1.8 0.8 %copy-done.2 = f32[2,4096]{1,0:T(2,128)S(1)} copy-done((f32[2,4096]{1,0:T(2,128)S(1)}, f32[2,4096]{1,0:T(2,128)}, u32[]{:S(2)}) %copy-start.2) | copy-done | bytes 32792
  2.5 0.0 copy-start.3
  2.5 0.8 %copy-done.3 = f32[2,4096]{1,0:T(2,128)S(1)} copy-done((f32[2,4096]{1,0:T(2,128)S(1)}, f32[2,4096]{1,0:T(2,128)}, u32[]{:S(2)}) %copy-start.3) | copy-done | bytes 32792
  3.3 0.0 copy-start.4
  3.3 0.7 %copy-done.4 = f32[4096]{0:T(1024)S(1)} copy-done((f32[4096]{0:T(1024)S(1)}, f32[4096]{0:T(1024)}, u32[]{:S(2)}) %copy-start.4) | copy-done | bytes 16408
  4.0 20.5 %shard_map.64 = bf16[128,4096]{1,0:T(8,128)(2,1)S(1)} custom-call(bf16[3,128,4096]{2,1,0:T(8,128)(2,1)} %x_hbm.1, f32[3,3,4096]{2,1,0:T(4,128)S(1)} %copy-done, f32[1,4096]{1,0:T(1,128)S(1)} %bitcast.1, f32[2,2,4096]{2,1,0:T(2,128)S(1)} %copy-done.1, f32[2,4096]{1,0:T(2,128)S(1)} %copy-done.2, f32[2,4096]{1,0:T(2,128)S(1)} %copy-done.3), custom_call_target="tpu_custom_call" | custom-call | flops 31457280 | bytes 4194304 | tf_op jit(solution)/shard_map/pallas_call | solution.py:426
  24.5 1.0 %copy.8 = bf16[128,4096]{1,0:T(8,128)(2,1)} copy(bf16[128,4096]{1,0:T(8,128)(2,1)S(1)} %shard_map.64) | data formatting | bytes 2097152
Async XLA Ops:
  0.0 0.9 %copy-start = (f32[3,3,4096]{2,1,0:T(4,128)S(1)}, f32[3,3,4096]{2,1,0:T(4,128)}, u32[]{:S(2)}) copy-start(f32[3,3,4096]{2,1,0:T(4,128)} %taps_hbm.1) | copy-start | bytes 442372
  0.9 0.8 %copy-start.1 = (f32[2,2,4096]{2,1,0:T(2,128)S(1)}, f32[2,2,4096]{2,1,0:T(2,128)}, u32[]{:S(2)}) copy-start(f32[2,2,4096]{2,1,0:T(2,128)} %res_hbm.1) | copy-start | bytes 196612
  1.8 0.8 %copy-start.2 = (f32[2,4096]{1,0:T(2,128)S(1)}, f32[2,4096]{1,0:T(2,128)}, u32[]{:S(2)}) copy-start(f32[2,4096]{1,0:T(2,128)} %ang_hbm.1) | copy-start | bytes 98308
  2.5 0.8 %copy-start.3 = (f32[2,4096]{1,0:T(2,128)S(1)}, f32[2,4096]{1,0:T(2,128)}, u32[]{:S(2)}) copy-start(f32[2,4096]{1,0:T(2,128)} %dec_hbm.1) | copy-start | bytes 98308
  3.3 0.7 %copy-start.4 = (f32[4096]{0:T(1024)S(1)}, f32[4096]{0:T(1024)}, u32[]{:S(2)}) copy-start(f32[4096]{0:T(1024)} %param.8) | copy-start | bytes 49156

commit v4 on v3

--- a/solution.py
+++ b/solution.py
@@ -14,8 +14,8 @@
 F32 = jnp.float32
 BF16 = jnp.bfloat16
 
-RE1, IM1, C1, C2, RE16, IM16, RE32, IM32, RE64, IM64, RE128, IM128, G0, G1, H1, H0R, H0I = range(17)
-TABLE_ROWS = 17
+RE1, IM1, C1, C2, RE16, IM16, RE32, IM32, RE64, IM64, RE128, IM128, G0, G1, H1, H0R, H0I, INVR, INVI = range(19)
+TABLE_ROWS = 19
 
 
 def square(re, im):
@@ -37,7 +37,7 @@
 def kernel(
     n, members,
     x_hbm, taps_hbm, skip_hbm, res_hbm, ang_hbm, dec_hbm, out_hbm,
-    xs, ordered, tail, taps, skip, res, ang, dec, to_chunks, to_rows, tab,
+    xs, delta, tail, taps, skip, res, ang, dec, to_chunks, to_rows, tab,
     halo_f32, halo_send, halo_recv, halo,
     prod, local, query, scan, t_send, t_in, c_out, c_in, g_out, g_in, outs,
     in_sems, kv_sems, out_sems, halo_sems, t_ssem, t_rsem, c_ssem, c_rsem, g_ssem, g_rsem, ready, halo_ready,
@@ -137,7 +137,10 @@
         tab[RE1, :, cols] = re
         tab[IM1, :, cols] = im
         tab[C1, :, cols] = 2.0 * re
-        tab[C2, :, cols] = -(re * re + im * im)
+        size = re * re + im * im
+        tab[C2, :, cols] = -size
+        tab[INVR, :, cols] = re / size
+        tab[INVI, :, cols] = -im / size
         tab[G0, :, cols] = r0
         tab[G1, :, cols] = -(r0 * re + r1 * im)
         tab[H1, :, cols] = -r1
@@ -176,35 +179,17 @@
 
     pl.when(me < n - 1)(halo_copy.start)
 
-    def order(i, part):
-        cols = pl.ds(pl.multiple_of(part * part_width, part_width), part_width)
-        ordered[i, :, cols] = jnp.dot(to_chunks[...], xs[i, :, cols], preferred_element_type=F32)
-
-    def order_kv(part, carry):
-        kv_copy(part).wait()
-        order(1, part)
-        order(2, part)
-        return carry
-
-    lax.fori_loop(0, kv_parts, order_kv, 0)
-
-    pl.when(me > 0)(halo_copy.wait_recv)
-    keep = me > 0
-    received = halo_recv[...].astype(F32)
-    received = jnp.where(keep, received, jnp.zeros_like(received))
-    halo[:, 0:half_width] = received[0:8]
-    halo[:, half_width:width] = received[8:16]
-
     sub = lax.broadcasted_iota(jnp.int32, (CHUNKS, WIDE), 0)
     first = sub == 0
 
     def param(which, pole, cols):
         return jnp.broadcast_to(tab[which, pole : pole + 1, cols], (CHUNKS, WIDE))
 
-    def short(i, cols):
-        at = [ordered[i, CHUNKS * r : CHUNKS * (r + 1), cols] for r in range(steps)]
-        before2 = jnp.where(first, halo[2 * i : 2 * i + 1, cols], pltpu.roll(at[steps - 2], 1, 0))
-        before1 = jnp.where(first, halo[2 * i + 1 : 2 * i + 2, cols], pltpu.roll(at[steps - 1], 1, 0))
+    def short(i, cols, edge):
+        x = jnp.dot(to_chunks[...], xs[i, :, cols], preferred_element_type=F32)
+        at = [x[CHUNKS * r : CHUNKS * (r + 1)] for r in range(steps)]
+        before2 = jnp.where(first, edge[0], pltpu.roll(at[steps - 2], 1, 0))
+        before1 = jnp.where(first, edge[1], pltpu.roll(at[steps - 1], 1, 0))
         at = [before2, before1] + at
         w = [jnp.broadcast_to(taps[tap, i : i + 1, cols], (CHUNKS, WIDE)) for tap in range(3)]
         return [w[0] * at[r] + w[1] * at[r + 1] + w[2] * at[r + 2] for r in range(steps)]
@@ -216,8 +201,8 @@
 
     def pass_a(b, carry):
         cols = pl.ds(pl.multiple_of(b * WIDE, WIDE), WIDE)
-        key = short(1, cols)
-        value = short(2, cols)
+        key = short(1, cols, (0.0, 0.0))
+        value = short(2, cols, (0.0, 0.0))
         c1 = [param(C1, pole, cols) for pole in range(2)]
         c2 = [param(C2, pole, cols) for pole in range(2)]
         now = [jnp.zeros((CHUNKS, WIDE), F32)] * 2
@@ -243,7 +228,45 @@
             t_send[owner, 1, pl.ds(pole, 1), there] = im[CHUNKS - 1 : CHUNKS]
         return carry
 
-    lax.fori_loop(0, blocks, pass_a, 0, unroll=2)
+    def part_a(part, carry):
+        kv_copy(part).wait()
+        each = part_width // WIDE
+        return lax.fori_loop(0, each, lambda b, c: pass_a(part * each + b, c), carry, unroll=2)
+
+    lax.fori_loop(0, kv_parts, part_a, 0)
+
+    pl.when(me > 0)(halo_copy.wait_recv)
+    keep = me > 0
+    received = halo_recv[...].astype(F32)
+    received = jnp.where(keep, received, jnp.zeros_like(received))
+    halo[:, 0:half_width] = received[0:8]
+    halo[:, half_width:width] = received[8:16]
+
+    def fix(owner, carry):
+        cols = pl.ds(pl.multiple_of(owner * quarter, quarter), quarter)
+        right = [1.0, 1.0]
+        for i in (1, 2):
+            x = xs[i, 0:16, cols].astype(F32)
+            x0, x1 = x[0:1], x[1:2]
+            h0, h1 = halo[2 * i : 2 * i + 1, cols], halo[2 * i + 1 : 2 * i + 2, cols]
+            w = [taps[tap, i : i + 1, cols] for tap in range(3)]
+            right[0] = right[0] * (w[0] * h0 + w[1] * h1 + w[2] * x0)
+            right[1] = right[1] * (w[0] * h1 + w[1] * x0 + w[2] * x1)
+        d0 = right[0] - prod[0:1, cols]
+        d1 = right[1] - prod[CHUNKS : CHUNKS + 1, cols]
+        prod[0:1, cols] = right[0]
+        prod[CHUNKS : CHUNKS + 1, cols] = right[1]
+        inv_r, inv_i = tab[INVR, :, cols], tab[INVI, :, cols]
+        re, im = d0 + inv_r * d1, inv_i * d1
+        re, im = inv_r * re - inv_i * im, inv_r * im + inv_i * re
+        delta[0, :, cols] = re
+        delta[1, :, cols] = im
+        wr, wi = tab[RE128, :, cols], tab[IM128, :, cols]
+        t_send[owner, 0] += wr * re - wi * im
+        t_send[owner, 1] += wr * im + wi * re
+        return carry
+
+    lax.fori_loop(0, members, fix, 0)
 
     def t_copy(source, target):
         return pltpu.make_async_remote_copy(
@@ -280,15 +303,9 @@
 
     q_copy.wait()
 
-    def order_q(part, carry):
-        order(0, part)
-        return carry
-
-    lax.fori_loop(0, kv_parts, order_q, 0)
-
     def pass_b(b, carry):
         cols = pl.ds(pl.multiple_of(b * WIDE, WIDE), WIDE)
-        for r, values in enumerate(short(0, cols)):
+        for r, values in enumerate(short(0, cols, (halo[0:1, cols], halo[1:2, cols]))):
             query[CHUNKS * r : CHUNKS * (r + 1), cols] = values
         return carry
 
@@ -375,6 +392,9 @@
             owner, there = message_place(b)
             cr = jnp.broadcast_to(c_in[owner, 0, pl.ds(pole, 1), there], (CHUNKS, WIDE))
             ci = jnp.broadcast_to(c_in[owner, 1, pl.ds(pole, 1), there], (CHUNKS, WIDE))
+            dr = jnp.broadcast_to(delta[0, pole : pole + 1, cols], (CHUNKS, WIDE))
+            di = jnp.broadcast_to(delta[1, pole : pole + 1, cols], (CHUNKS, WIDE))
+            cr, ci = jnp.where(first, cr, cr + dr), jnp.where(first, ci, ci + di)
             for bit, wr, wi in ((1, RE16, IM16), (2, RE32, IM32), (4, RE64, IM64)):
                 wr, wi = param(wr, pole, cols), param(wi, pole, cols)
                 has = (sub & bit) > 0
@@ -393,7 +413,7 @@
             for pole in range(2):
                 now[pole], old[pole] = c2[pole] * old[pole] + c1[pole] * now[pole], now[pole]
         gated = jnp.concatenate(done, axis=0).astype(BF16)
-        outs[:, cols] = jnp.dot(to_rows[...], gated, preferred_element_type=F32).astype(BF16)
+        outs[:, cols] = jnp.dot(to_rows[...], gated, preferred_element_type=F32)
         out_copy(b).start()
         return carry
 
@@ -425,12 +445,12 @@
         vmem = pltpu.VMEM
         return pl.pallas_call(
             functools.partial(kernel, n, members),
-            out_shape=jax.ShapeDtypeStruct((rows, width), BF16),
+            out_shape=jax.ShapeDtypeStruct((rows, width), F32),
             in_specs=[pl.BlockSpec(memory_space=pl.ANY)] * 6,
             out_specs=pl.BlockSpec(memory_space=pl.ANY),
             scratch_shapes=[
                 vmem((3, rows, width), BF16),
-                vmem((3, rows, width), F32),
+                vmem((2, 2, width), F32),
                 vmem((3, 16, width), BF16),
                 vmem(short_taps.shape, F32),
                 vmem((1, width), F32),
@@ -454,7 +474,7 @@
                 vmem((members, 2, 2, quarter), F32),
                 vmem((2, 2, quarter), F32),
                 vmem((groups, 2, 2, quarter), F32),
-                vmem((rows, width), BF16),
+                vmem((rows, width), F32),
                 dma((7,)),
                 dma((kv_parts,)),
                 dma((width // WIDE,)),
@@ -469,12 +489,12 @@
                 pltpu.SemaphoreType.REGULAR,
             ],
             compiler_params=pltpu.CompilerParams(
-                collective_id=0, has_side_effects=True, vmem_limit_bytes=52 * 1024 * 1024
+                collective_id=0, has_side_effects=True, vmem_limit_bytes=63 * 1024 * 1024
             ),
             cost_estimate=pl.CostEstimate(
                 flops=60 * rows * width, bytes_accessed=8 * rows * width, transcendentals=2 * width
             ),
-        )(projected, short_taps, skip_gain.reshape(1, width), residues, pole_angles, decay_rates)
+        )(projected, short_taps, skip_gain.reshape(1, width), residues, pole_angles, decay_rates).astype(BF16)
 
     return jax.shard_map(
         on_device,

time: 25.8 us -> 20.9 us (0.81)
  local copies, waits for them, and re-layouts: 4.97 us -> 0 us
  other arithmetic: 0 us -> 2.69 us
  Pallas kernels: 20.5 us -> 18.1 us
    unnamed x11 -> x0, local copies, waits for them, and re-layouts: 4.97 us -> none
    convert_element_type x0 -> x1, other arithmetic: none -> 2.69 us  [on_device(): return pl.pallas_call(functools.partial(kernel, n, members), out_shape=ja...]
    pallas_call x1, Pallas kernels: 20.5 us -> 18.1 us  [on_device(): pl.pallas_call(functools.partial(kernel, n, members), out_shape=jax.Shape...]
where the time goes in v4:
time: 20.9 us; the launch traced here: 20.8 us
  Pallas kernels  18.1 us (87%)
  other arithmetic  2.69 us (13%)
    pallas_call x1, Pallas kernels, on_device(): pl.pallas_call(functools.partial(kernel, n, members), out_shape=jax.Shape...  18.1 us
    convert_element_type x1, other arithmetic, on_device(): return pl.pallas_call(functools.partial(kernel, n, members), out_shape=ja...  2.69 us

profile of v4, /device:TPU:25, one launch (start us, length us, event | category | flops | bytes accessed | tf_op | source)
XLA Modules:
  0.0 20.8 jit_solution(6347750708652992164)
XLA Ops:
  0.0 18.1 %shard_map.64 = f32[128,4096]{1,0:T(8,128)} custom-call(bf16[3,128,4096]{2,1,0:T(8,128)(2,1)} %x_hbm.1, f32[3,3,4096]{2,1,0:T(4,128)} %taps_hbm.1, f32[1,4096]{1,0:T(1,128)} %bitcast.1, f32[2,2,4096]{2,1,0:T(2,128)} %res_hbm.1, f32[2,4096]{1,0:T(2,128)} %ang_hbm.1, f32[2,4096]{1,0:T(2,128)} %dec_hbm.1), custom_call_target="tpu_custom_call" | custom-call | flops 31457280 | bytes 4194304 | tf_op jit(solution)/shard_map/pallas_call | solution.py:446
  18.1 2.7 %convert_element_type.3 = bf16[128,4096]{1,0:T(8,128)(2,1)} convert(f32[128,4096]{1,0:T(8,128)} %shard_map.64) | non-fusion elementwise | flops 524288 | bytes 3145728 | tf_op jit(solution)/shard_map/convert_element_type | solution.py:497

commit v5 on v4

--- a/solution.py
+++ b/solution.py
@@ -37,9 +37,9 @@
 def kernel(
     n, members,
     x_hbm, taps_hbm, skip_hbm, res_hbm, ang_hbm, dec_hbm, out_hbm,
-    xs, delta, tail, taps, skip, res, ang, dec, to_chunks, to_rows, tab,
+    xs, delta, tail, taps, skip, res, ang, dec, to_chunks, tab,
     halo_f32, halo_send, halo_recv, halo,
-    prod, local, query, scan, t_send, t_in, c_out, c_in, g_out, g_in, outs,
+    prod, local, query, scan, state, spin, carried, t_send, t_in, c_out, c_in, g_out, g_in, outs,
     in_sems, kv_sems, out_sems, halo_sems, t_ssem, t_rsem, c_ssem, c_rsem, g_ssem, g_rsem, ready, halo_ready,
 ):
     rows, width = xs.shape[1], xs.shape[2]
@@ -49,6 +49,8 @@
     kv_parts = kv_sems.shape[0]
     part_width = width // kv_parts
     quarter = width // members
+    pieces = quarter // WIDE
+    half = 2 * pieces
     me = lax.axis_index("seq")
     place = lax.rem(me, members)
     base = me - place
@@ -107,7 +109,6 @@
     i0 = lax.broadcasted_iota(jnp.int32, (rows, rows), 0)
     i1 = lax.broadcasted_iota(jnp.int32, (rows, rows), 1)
     to_chunks[...] = jnp.where(i1 == (i0 & (CHUNKS - 1)) * steps + (i0 >> 3), 1.0, 0.0).astype(BF16)
-    to_rows[...] = jnp.where(i0 == (i1 & (CHUNKS - 1)) * steps + (i1 >> 3), 1.0, 0.0).astype(BF16)
 
     tail_copy.wait()
     for i in range(3):
@@ -195,9 +196,8 @@
         return [w[0] * at[r] + w[1] * at[r + 1] + w[2] * at[r + 2] for r in range(steps)]
 
     def message_place(b):
-        each = quarter // WIDE
-        owner = b // each
-        return owner, pl.ds(pl.multiple_of((b - owner * each) * WIDE, WIDE), WIDE)
+        owner = b // pieces
+        return owner, 2 * (b - owner * pieces)
 
     def pass_a(b, carry):
         cols = pl.ds(pl.multiple_of(b * WIDE, WIDE), WIDE)
@@ -223,9 +223,9 @@
                 re, im = re + (wr * pr - wi * pi), im + (wr * pi + wi * pr)
             scan[2 * pole, :, cols] = jnp.where(first, 0.0, pltpu.roll(re, 1, 0))
             scan[2 * pole + 1, :, cols] = jnp.where(first, 0.0, pltpu.roll(im, 1, 0))
-            owner, there = message_place(b)
-            t_send[owner, 0, pl.ds(pole, 1), there] = re[CHUNKS - 1 : CHUNKS]
-            t_send[owner, 1, pl.ds(pole, 1), there] = im[CHUNKS - 1 : CHUNKS]
+            owner, row = message_place(b)
+            state[owner, pl.ds(row + pole, 1), :] = re[CHUNKS - 1 : CHUNKS]
+            state[owner, pl.ds(half + row + pole, 1), :] = im[CHUNKS - 1 : CHUNKS]
         return carry
 
     def part_a(part, carry):
@@ -262,8 +262,12 @@
         delta[0, :, cols] = re
         delta[1, :, cols] = im
         wr, wi = tab[RE128, :, cols], tab[IM128, :, cols]
-        t_send[owner, 0] += wr * re - wi * im
-        t_send[owner, 1] += wr * im + wi * re
+        add = (wr * re - wi * im, wr * im + wi * re)
+        for part in range(2):
+            for piece in range(pieces):
+                row = part * half + 2 * piece
+                state[owner, row : row + 2, :] += add[part][:, piece * WIDE : (piece + 1) * WIDE]
+        t_send[owner] = state[owner].astype(BF16)
         return carry
 
     lax.fori_loop(0, members, fix, 0)
@@ -330,21 +334,21 @@
     lax.fori_loop(0, blocks, pass_b, 0, unroll=2)
 
     t_in[pl.ds(place, 1)] = t_send[pl.ds(place, 1)]
+    for piece in range(pieces):
+        cols = pl.ds(pl.multiple_of(place * quarter + piece * WIDE, WIDE), WIDE)
+        spin[0, 2 * piece : 2 * piece + 2, :] = tab[RE128, :, cols]
+        spin[1, 2 * piece : 2 * piece + 2, :] = tab[IM128, :, cols]
     for step in range(1, members):
         t_copy(peer(step), place).wait_recv()
 
-    mine = pl.ds(pl.multiple_of(place * quarter, quarter), quarter)
-    wr, wi = tab[RE128, :, mine], tab[IM128, :, mine]
-    re = im = jnp.zeros((2, quarter), F32)
+    wr, wi = spin[0], spin[1]
+    re = im = jnp.zeros((half, WIDE), F32)
     inside = []
     for member in range(members):
         inside.append((re, im))
-        re, im = (
-            wr * re - wi * im + t_in[member, 0],
-            wr * im + wi * re + t_in[member, 1],
-        )
-    g_out[0] = re
-    g_out[1] = im
+        ended = t_in[member].astype(F32)
+        re, im = wr * re - wi * im + ended[:half], wr * im + wi * re + ended[half:]
+    g_out[...] = jnp.concatenate([re, im], axis=0).astype(BF16)
 
     def send_g(ahead):
         pl.semaphore_wait(ready.at[ahead], 1)
@@ -361,13 +365,15 @@
     def add_group(source, state):
         re, im = state
         g_copy(source, 1).wait_recv()
-        return gr * re - gi * im + g_in[source, 0], gr * im + gi * re + g_in[source, 1]
-
-    zero = jnp.zeros((2, quarter), F32)
+        ended = g_in[source].astype(F32)
+        return gr * re - gi * im + ended[:half], gr * im + gi * re + ended[half:]
+
+    zero = jnp.zeros((half, WIDE), F32)
     re, im = lax.fori_loop(0, group, add_group, (zero, zero))
     for member in range(members):
-        c_out[member, 0] = inside[member][0] + re
-        c_out[member, 1] = inside[member][1] + im
+        c_out[member] = jnp.concatenate(
+            [inside[member][0] + re, inside[member][1] + im], axis=0
+        ).astype(BF16)
         re, im = wr * re - wi * im, wr * im + wi * re
 
     for step in range(1, members):
@@ -378,6 +384,7 @@
 
     for step in range(1, members):
         c_copy(peer(step), place).wait_recv()
+    carried[...] = c_in[...].astype(F32)
 
     def out_copy(b):
         cols = pl.ds(pl.multiple_of(b * WIDE, WIDE), WIDE)
@@ -389,9 +396,9 @@
         c2 = [param(C2, pole, cols) for pole in range(2)]
         now, old = [], []
         for pole in range(2):
-            owner, there = message_place(b)
-            cr = jnp.broadcast_to(c_in[owner, 0, pl.ds(pole, 1), there], (CHUNKS, WIDE))
-            ci = jnp.broadcast_to(c_in[owner, 1, pl.ds(pole, 1), there], (CHUNKS, WIDE))
+            owner, row = message_place(b)
+            cr = jnp.broadcast_to(carried[owner, pl.ds(row + pole, 1), :], (CHUNKS, WIDE))
+            ci = jnp.broadcast_to(carried[owner, pl.ds(half + row + pole, 1), :], (CHUNKS, WIDE))
             dr = jnp.broadcast_to(delta[0, pole : pole + 1, cols], (CHUNKS, WIDE))
             di = jnp.broadcast_to(delta[1, pole : pole + 1, cols], (CHUNKS, WIDE))
             cr, ci = jnp.where(first, cr, cr + dr), jnp.where(first, ci, ci + di)
@@ -413,7 +420,7 @@
             for pole in range(2):
                 now[pole], old[pole] = c2[pole] * old[pole] + c1[pole] * now[pole], now[pole]
         gated = jnp.concatenate(done, axis=0).astype(BF16)
-        outs[:, cols] = jnp.dot(to_rows[...], gated, preferred_element_type=F32)
+        outs[:, cols] = gated
         out_copy(b).start()
         return carry
 
@@ -432,6 +439,33 @@
     pl.when(me < n - 1)(halo_copy.wait_send)
 
 
+def rows_kernel(x_hbm, out_hbm, xs, outs, in_sems, out_sems):
+    rows, width = xs.shape
+    steps = rows // CHUNKS
+    parts = in_sems.shape[0]
+    each = width // parts
+    places = [pl.ds(part * each, each) for part in range(parts)]
+    ins = [
+        pltpu.make_async_copy(x_hbm.at[:, cols], xs.at[:, cols], in_sems.at[part])
+        for part, cols in enumerate(places)
+    ]
+    backs = [
+        pltpu.make_async_copy(outs.at[:, cols], out_hbm.at[:, cols], out_sems.at[part])
+        for part, cols in enumerate(places)
+    ]
+    for copy in ins:
+        copy.start()
+    i0 = lax.broadcasted_iota(jnp.int32, (rows, rows), 0)
+    i1 = lax.broadcasted_iota(jnp.int32, (rows, rows), 1)
+    to_rows = jnp.where(i0 == (i1 & (CHUNKS - 1)) * steps + (i1 >> 3), 1.0, 0.0).astype(BF16)
+    for part, cols in enumerate(places):
+        ins[part].wait()
+        outs[:, cols] = jnp.dot(to_rows, xs[:, cols], preferred_element_type=F32).astype(BF16)
+        backs[part].start()
+    for copy in backs:
+        copy.wait()
+
+
 def solution(mesh):
     n = mesh.shape["seq"]
 
@@ -440,12 +474,13 @@
         members = math.gcd(n, 4)
         quarter = width // members
         groups = n // members
+        message = 4 * quarter // WIDE
         kv_parts = 4
         dma = pltpu.SemaphoreType.DMA
         vmem = pltpu.VMEM
-        return pl.pallas_call(
+        in_chunks = pl.pallas_call(
             functools.partial(kernel, n, members),
-            out_shape=jax.ShapeDtypeStruct((rows, width), F32),
+            out_shape=jax.ShapeDtypeStruct((rows, width), BF16),
             in_specs=[pl.BlockSpec(memory_space=pl.ANY)] * 6,
             out_specs=pl.BlockSpec(memory_space=pl.ANY),
             scratch_shapes=[
@@ -458,7 +493,6 @@
                 vmem(pole_angles.shape, F32),
                 vmem(decay_rates.shape, F32),
                 vmem((rows, rows), BF16),
-                vmem((rows, rows), BF16),
                 vmem((TABLE_ROWS, 2, width), F32),
                 vmem((16, width // 2), F32),
                 vmem((16, width // 2), BF16),
@@ -468,13 +502,16 @@
                 vmem((rows, width), F32),
                 vmem((rows, width), F32),
                 vmem((4, CHUNKS, width), F32),
-                vmem((members, 2, 2, quarter), F32),
-                vmem((members, 2, 2, quarter), F32),
-                vmem((members, 2, 2, quarter), F32),
-                vmem((members, 2, 2, quarter), F32),
-                vmem((2, 2, quarter), F32),
-                vmem((groups, 2, 2, quarter), F32),
-                vmem((rows, width), F32),
+                vmem((members, message, WIDE), F32),
+                vmem((2, message // 2, WIDE), F32),
+                vmem((members, message, WIDE), F32),
+                vmem((members, message, WIDE), BF16),
+                vmem((members, message, WIDE), BF16),
+                vmem((members, message, WIDE), BF16),
+                vmem((members, message, WIDE), BF16),
+                vmem((message, WIDE), BF16),
+                vmem((groups, message, WIDE), BF16),
+                vmem((rows, width), BF16),
                 dma((7,)),
                 dma((kv_parts,)),
                 dma((width // WIDE,)),
@@ -494,7 +531,24 @@
             cost_estimate=pl.CostEstimate(
                 flops=60 * rows * width, bytes_accessed=8 * rows * width, transcendentals=2 * width
             ),
-        )(projected, short_taps, skip_gain.reshape(1, width), residues, pole_angles, decay_rates).astype(BF16)
+        )(projected, short_taps, skip_gain.reshape(1, width), residues, pole_angles, decay_rates)
+        parts = 8
+        return pl.pallas_call(
+            rows_kernel,
+            out_shape=jax.ShapeDtypeStruct((rows, width), BF16),
+            in_specs=[pl.BlockSpec(memory_space=pl.ANY)],
+            out_specs=pl.BlockSpec(memory_space=pl.ANY),
+            scratch_shapes=[
+                vmem((rows, width), BF16),
+                vmem((rows, width), BF16),
+                dma((parts,)),
+                dma((parts,)),
+            ],
+            compiler_params=pltpu.CompilerParams(vmem_limit_bytes=63 * 1024 * 1024),
+            cost_estimate=pl.CostEstimate(
+                flops=2 * rows * rows * width, bytes_accessed=4 * rows * width, transcendentals=0
+            ),
+        )(in_chunks)
 
     return jax.shard_map(
         on_device,

time: 20.9 us -> 19.8 us (0.947)
  other arithmetic: 2.69 us -> 0 us
  Pallas kernels: 18.1 us -> 19.6 us
    pallas_call x0 -> x1, Pallas kernels: none -> 3.11 us  [on_device(): pl.pallas_call(rows_kernel, out_shape=jax.ShapeDtypeStruct((rows, width),...]
    convert_element_type x1 -> x0, other arithmetic: 2.69 us -> none  [on_device(): return pl.pallas_call(functools.partial(kernel, n, members), out_shape=ja...]
    pallas_call x1, Pallas kernels: 18.1 us -> 16.5 us  [on_device(): pl.pallas_call(functools.partial(kernel, n, members), out_shape=jax.Shape...]
where the time goes in v5:
time: 19.8 us; the launch traced here: 19.6 us
  Pallas kernels  19.6 us (99%)
    pallas_call x1, Pallas kernels, on_device(): pl.pallas_call(functools.partial(kernel, n, members), out_shape=jax.Shape...  16.5 us
    pallas_call x1, Pallas kernels, on_device(): pl.pallas_call(rows_kernel, out_shape=jax.ShapeDtypeStruct((rows, width),...  3.11 us

profile of v5, /device:TPU:25, one launch (start us, length us, event | category | flops | bytes accessed | tf_op | source)
XLA Modules:
  0.0 19.6 jit_solution(14035662800230763667)
XLA Ops:
  0.0 16.5 %shard_map.64.x_hbm = bf16[128,4096]{1,0:T(8,128)(2,1)} custom-call(bf16[3,128,4096]{2,1,0:T(8,128)(2,1)} %x_hbm.1, f32[3,3,4096]{2,1,0:T(4,128)} %taps_hbm.1, f32[1,4096]{1,0:T(1,128)} %bitcast.1, f32[2,2,4096]{2,1,0:T(2,128)} %res_hbm.1, f32[2,4096]{1,0:T(2,128)} %ang_hbm.1, f32[2,4096]{1,0:T(2,128)} %dec_hbm.1), custom_call_target="tpu_custom_call" | custom-call | flops 31457280 | bytes 4194304 | tf_op jit(solution)/shard_map/pallas_call | solution.py:481
  16.5 3.1 %shard_map.65 = bf16[128,4096]{1,0:T(8,128)(2,1)} custom-call(bf16[128,4096]{1,0:T(8,128)(2,1)} %shard_map.64.x_hbm), custom_call_target="tpu_custom_call" | custom-call | flops 134217728 | bytes 2097152 | tf_op jit(solution)/shard_map/pallas_call | solution.py:536

commit v6 on v5

--- a/solution.py
+++ b/solution.py
@@ -37,7 +37,7 @@
 def kernel(
     n, members,
     x_hbm, taps_hbm, skip_hbm, res_hbm, ang_hbm, dec_hbm, out_hbm,
-    xs, delta, tail, taps, skip, res, ang, dec, to_chunks, tab,
+    xs, delta, tail, taps, skip, res, ang, dec, to_chunks, to_rows, tab,
     halo_f32, halo_send, halo_recv, halo,
     prod, local, query, scan, state, spin, carried, t_send, t_in, c_out, c_in, g_out, g_in, outs,
     in_sems, kv_sems, out_sems, halo_sems, t_ssem, t_rsem, c_ssem, c_rsem, g_ssem, g_rsem, ready, halo_ready,
@@ -109,6 +109,8 @@
     i0 = lax.broadcasted_iota(jnp.int32, (rows, rows), 0)
     i1 = lax.broadcasted_iota(jnp.int32, (rows, rows), 1)
     to_chunks[...] = jnp.where(i1 == (i0 & (CHUNKS - 1)) * steps + (i0 >> 3), 1.0, 0.0).astype(BF16)
+
+    to_rows[...] = jnp.where(i0 == (i1 & (CHUNKS - 1)) * steps + (i1 >> 3), 1.0, 0.0).astype(BF16)
 
     tail_copy.wait()
     for i in range(3):
@@ -420,7 +422,7 @@
             for pole in range(2):
                 now[pole], old[pole] = c2[pole] * old[pole] + c1[pole] * now[pole], now[pole]
         gated = jnp.concatenate(done, axis=0).astype(BF16)
-        outs[:, cols] = gated
+        outs[:, cols] = jnp.dot(to_rows[...], gated, preferred_element_type=F32).astype(BF16)
         out_copy(b).start()
         return carry
 
@@ -437,33 +439,6 @@
         c_copy(place, peer(step)).wait_send()
     in_later_groups(lambda ahead: g_copy(group, ahead).wait_send())
     pl.when(me < n - 1)(halo_copy.wait_send)
-
-
-def rows_kernel(x_hbm, out_hbm, xs, outs, in_sems, out_sems):
-    rows, width = xs.shape
-    steps = rows // CHUNKS
-    parts = in_sems.shape[0]
-    each = width // parts
-    places = [pl.ds(part * each, each) for part in range(parts)]
-    ins = [
-        pltpu.make_async_copy(x_hbm.at[:, cols], xs.at[:, cols], in_sems.at[part])
-        for part, cols in enumerate(places)
-    ]
-    backs = [
-        pltpu.make_async_copy(outs.at[:, cols], out_hbm.at[:, cols], out_sems.at[part])
-        for part, cols in enumerate(places)
-    ]
-    for copy in ins:
-        copy.start()
-    i0 = lax.broadcasted_iota(jnp.int32, (rows, rows), 0)
-    i1 = lax.broadcasted_iota(jnp.int32, (rows, rows), 1)
-    to_rows = jnp.where(i0 == (i1 & (CHUNKS - 1)) * steps + (i1 >> 3), 1.0, 0.0).astype(BF16)
-    for part, cols in enumerate(places):
-        ins[part].wait()
-        outs[:, cols] = jnp.dot(to_rows, xs[:, cols], preferred_element_type=F32).astype(BF16)
-        backs[part].start()
-    for copy in backs:
-        copy.wait()
 
 
 def solution(mesh):
@@ -478,9 +453,9 @@
         kv_parts = 4
         dma = pltpu.SemaphoreType.DMA
         vmem = pltpu.VMEM
-        in_chunks = pl.pallas_call(
+        return pl.pallas_call(
             functools.partial(kernel, n, members),
-            out_shape=jax.ShapeDtypeStruct((rows, width), BF16),
+            out_shape=pltpu.VMEM((rows, width), BF16),
             in_specs=[pl.BlockSpec(memory_space=pl.ANY)] * 6,
             out_specs=pl.BlockSpec(memory_space=pl.ANY),
             scratch_shapes=[
@@ -492,6 +467,7 @@
                 vmem(residues.shape, F32),
                 vmem(pole_angles.shape, F32),
                 vmem(decay_rates.shape, F32),
+                vmem((rows, rows), BF16),
                 vmem((rows, rows), BF16),
                 vmem((TABLE_ROWS, 2, width), F32),
                 vmem((16, width // 2), F32),
@@ -526,29 +502,19 @@
                 pltpu.SemaphoreType.REGULAR,
             ],
             compiler_params=pltpu.CompilerParams(
-                collective_id=0, has_side_effects=True, vmem_limit_bytes=63 * 1024 * 1024
+                collective_id=0, has_side_effects=True, vmem_limit_bytes=40 * 1024 * 1024
             ),
             cost_estimate=pl.CostEstimate(
                 flops=60 * rows * width, bytes_accessed=8 * rows * width, transcendentals=2 * width
             ),
-        )(projected, short_taps, skip_gain.reshape(1, width), residues, pole_angles, decay_rates)
-        parts = 8
-        return pl.pallas_call(
-            rows_kernel,
-            out_shape=jax.ShapeDtypeStruct((rows, width), BF16),
-            in_specs=[pl.BlockSpec(memory_space=pl.ANY)],
-            out_specs=pl.BlockSpec(memory_space=pl.ANY),
-            scratch_shapes=[
-                vmem((rows, width), BF16),
-                vmem((rows, width), BF16),
-                dma((parts,)),
-                dma((parts,)),
-            ],
-            compiler_params=pltpu.CompilerParams(vmem_limit_bytes=63 * 1024 * 1024),
-            cost_estimate=pl.CostEstimate(
-                flops=2 * rows * rows * width, bytes_accessed=4 * rows * width, transcendentals=0
-            ),
-        )(in_chunks)
+        )(
+            *[
+                pltpu.with_memory_space_constraint(x, pltpu.HBM)
+                for x in (
+                    projected, short_taps, skip_gain.reshape(1, width), residues, pole_angles, decay_rates
+                )
+            ]
+        )
 
     return jax.shard_map(
         on_device,

time: 19.8 us -> 19.7 us (level)
  Pallas kernels: 19.6 us -> 18.6 us
  local copies, waits for them, and re-layouts: 0 us -> 0.97 us
    pallas_call x2 -> x1, Pallas kernels: 19.6 us -> 18.6 us  [on_device(): pl.pallas_call(functools.partial(kernel, n, members), out_shape=pltpu.VME...]
    unnamed x0 -> x1, local copies, waits for them, and re-layouts: none -> 0.97 us
where the time goes in v6:
time: 19.7 us; the launch traced here: 19.6 us
  Pallas kernels  18.6 us (94%)
  local copies, waits for them, and re-layouts  0.97 us (5%)
    pallas_call x1, Pallas kernels, on_device(): pl.pallas_call(functools.partial(kernel, n, members), out_shape=pltpu.VME...  18.6 us
    unnamed x1, local copies, waits for them, and re-layouts  0.97 us

profile of v6, /device:TPU:25, one launch (start us, length us, event | category | flops | bytes accessed | tf_op | source)
XLA Modules:
  0.0 19.6 jit_solution(16193133476197265682)
XLA Ops:
  0.0 18.6 %shard_map.64 = bf16[128,4096]{1,0:T(8,128)(2,1)S(1)} custom-call(bf16[3,128,4096]{2,1,0:T(8,128)(2,1)} %x_hbm.1, f32[3,3,4096]{2,1,0:T(4,128)} %taps_hbm.1, f32[1,4096]{1,0:T(1,128)} %bitcast.1, f32[2,2,4096]{2,1,0:T(2,128)} %res_hbm.1, f32[2,4096]{1,0:T(2,128)} %ang_hbm.1, f32[2,4096]{1,0:T(2,128)} %dec_hbm.1), custom_call_target="tpu_custom_call" | custom-call | flops 31457280 | bytes 4194304 | tf_op jit(solution)/shard_map/pallas_call | solution.py:456
  18.6 1.0 %copy.8 = bf16[128,4096]{1,0:T(8,128)(2,1)} copy(bf16[128,4096]{1,0:T(8,128)(2,1)S(1)} %shard_map.64) | data formatting | bytes 2097152

commit v7 on v6

--- a/solution.py
+++ b/solution.py
@@ -37,7 +37,7 @@
 def kernel(
     n, members,
     x_hbm, taps_hbm, skip_hbm, res_hbm, ang_hbm, dec_hbm, out_hbm,
-    xs, delta, tail, taps, skip, res, ang, dec, to_chunks, to_rows, tab,
+    xs, even, odd, gated_even, gated_odd, delta, tail, taps, skip, res, ang, dec, to_chunks, to_rows, tab,
     halo_f32, halo_send, halo_recv, halo,
     prod, local, query, scan, state, spin, carried, t_send, t_in, c_out, c_in, g_out, g_in, outs,
     in_sems, kv_sems, out_sems, halo_sems, t_ssem, t_rsem, c_ssem, c_rsem, g_ssem, g_rsem, ready, halo_ready,
@@ -188,9 +188,31 @@
     def param(which, pole, cols):
         return jnp.broadcast_to(tab[which, pole : pole + 1, cols], (CHUNKS, WIDE))
 
-    def short(i, cols, edge):
-        x = jnp.dot(to_chunks[...], xs[i, :, cols], preferred_element_type=F32)
-        at = [x[CHUNKS * r : CHUNKS * (r + 1)] for r in range(steps)]
+    def block(b):
+        return pl.ds(pl.multiple_of(b * WIDE, WIDE), WIDE)
+
+    def order(b, projections, buffer):
+        for slot, i in enumerate(projections):
+            buffer[slot] = jnp.dot(to_chunks[...], xs[i, :, block(b)], preferred_element_type=F32)
+
+    def ordered_blocks(projections, work):
+        order(0, projections, even)
+
+        def two(pair, carry):
+            b = 2 * pair
+            order(b + 1, projections, odd)
+            work(b, even)
+            order(b + 2, projections, even)
+            work(b + 1, odd)
+            return carry
+
+        lax.fori_loop(0, blocks // 2 - 1, two, 0)
+        order(blocks - 1, projections, odd)
+        work(blocks - 2, even)
+        work(blocks - 1, odd)
+
+    def short(i, x, cols, edge):
+        at = [x[CHUNKS * r : CHUNKS * (r + 1), :] for r in range(steps)]
         before2 = jnp.where(first, edge[0], pltpu.roll(at[steps - 2], 1, 0))
         before1 = jnp.where(first, edge[1], pltpu.roll(at[steps - 1], 1, 0))
         at = [before2, before1] + at
@@ -201,10 +223,10 @@
         owner = b // pieces
         return owner, 2 * (b - owner * pieces)
 
-    def pass_a(b, carry):
+    def pass_a(b, buffer):
         cols = pl.ds(pl.multiple_of(b * WIDE, WIDE), WIDE)
-        key = short(1, cols, (0.0, 0.0))
-        value = short(2, cols, (0.0, 0.0))
+        key = short(1, buffer.at[0], cols, (0.0, 0.0))
+        value = short(2, buffer.at[1], cols, (0.0, 0.0))
         c1 = [param(C1, pole, cols) for pole in range(2)]
         c2 = [param(C2, pole, cols) for pole in range(2)]
         now = [jnp.zeros((CHUNKS, WIDE), F32)] * 2
@@ -228,14 +250,10 @@
             owner, row = message_place(b)
             state[owner, pl.ds(row + pole, 1), :] = re[CHUNKS - 1 : CHUNKS]
             state[owner, pl.ds(half + row + pole, 1), :] = im[CHUNKS - 1 : CHUNKS]
-        return carry
-
-    def part_a(part, carry):
+
+    for part in range(kv_parts):
         kv_copy(part).wait()
-        each = part_width // WIDE
-        return lax.fori_loop(0, each, lambda b, c: pass_a(part * each + b, c), carry, unroll=2)
-
-    lax.fori_loop(0, kv_parts, part_a, 0)
+    ordered_blocks((1, 2), pass_a)
 
     pl.when(me > 0)(halo_copy.wait_recv)
     keep = me > 0
@@ -309,11 +327,11 @@
 
     q_copy.wait()
 
-    def pass_b(b, carry):
-        cols = pl.ds(pl.multiple_of(b * WIDE, WIDE), WIDE)
-        for r, values in enumerate(short(0, cols, (halo[0:1, cols], halo[1:2, cols]))):
+    def pass_b(b, buffer):
+        cols = block(b)
+        edge = (halo[0:1, cols], halo[1:2, cols])
+        for r, values in enumerate(short(0, buffer.at[0], cols, edge)):
             query[CHUNKS * r : CHUNKS * (r + 1), cols] = values
-        return carry
 
     def pass_b2(b, carry):
         cols = pl.ds(pl.multiple_of(b * WIDE, WIDE), WIDE)
@@ -333,7 +351,7 @@
             before = p
         return carry
 
-    lax.fori_loop(0, blocks, pass_b, 0, unroll=2)
+    ordered_blocks((0,), pass_b)
 
     t_in[pl.ds(place, 1)] = t_send[pl.ds(place, 1)]
     for piece in range(pieces):
@@ -392,7 +410,7 @@
         cols = pl.ds(pl.multiple_of(b * WIDE, WIDE), WIDE)
         return pltpu.make_async_copy(outs.at[:, cols], out_hbm.at[:, cols], out_sems.at[b])
 
-    def pass_c(b, carry):
+    def pass_c(b, buffer):
         cols = pl.ds(pl.multiple_of(b * WIDE, WIDE), WIDE)
         c1 = [param(C1, pole, cols) for pole in range(2)]
         c2 = [param(C2, pole, cols) for pole in range(2)]
@@ -421,12 +439,28 @@
             done.append(query[at, cols] * (local[at, cols] + (now[0] + now[1])))
             for pole in range(2):
                 now[pole], old[pole] = c2[pole] * old[pole] + c1[pole] * now[pole], now[pole]
-        gated = jnp.concatenate(done, axis=0).astype(BF16)
-        outs[:, cols] = jnp.dot(to_rows[...], gated, preferred_element_type=F32).astype(BF16)
+        buffer[...] = jnp.concatenate(done, axis=0).astype(BF16)
+
+    def give(b, buffer):
+        outs[:, block(b)] = jnp.dot(
+            to_rows[...], buffer[...], preferred_element_type=F32
+        ).astype(BF16)
         out_copy(b).start()
+
+    pass_c(0, gated_even)
+
+    def two_out(pair, carry):
+        b = 2 * pair
+        pass_c(b + 1, gated_odd)
+        give(b, gated_even)
+        pass_c(b + 2, gated_even)
+        give(b + 1, gated_odd)
         return carry
 
-    lax.fori_loop(0, blocks, pass_c, 0, unroll=2)
+    lax.fori_loop(0, blocks // 2 - 1, two_out, 0)
+    pass_c(blocks - 1, gated_odd)
+    give(blocks - 2, gated_even)
+    give(blocks - 1, gated_odd)
 
     def wait_out(b, carry):
         out_copy(b).wait()
@@ -460,6 +494,10 @@
             out_specs=pl.BlockSpec(memory_space=pl.ANY),
             scratch_shapes=[
                 vmem((3, rows, width), BF16),
+                vmem((2, rows, WIDE), F32),
+                vmem((2, rows, WIDE), F32),
+                vmem((rows, WIDE), BF16),
+                vmem((rows, WIDE), BF16),
                 vmem((2, 2, width), F32),
                 vmem((3, 16, width), BF16),
                 vmem(short_taps.shape, F32),

time: 19.7 us -> 19 us (0.964)
  Pallas kernels: 18.6 us -> 17.9 us
    pallas_call x1, Pallas kernels: 18.6 us -> 17.9 us  [on_device(): pl.pallas_call(functools.partial(kernel, n, members), out_shape=pltpu.VME...]
where the time goes in v7:
time: 19 us; the launch traced here: 18.9 us
  Pallas kernels  17.9 us (94%)
  local copies, waits for them, and re-layouts  0.97 us (5%)
    pallas_call x1, Pallas kernels, on_device(): pl.pallas_call(functools.partial(kernel, n, members), out_shape=pltpu.VME...  17.9 us
    unnamed x1, local copies, waits for them, and re-layouts  0.97 us

profile of v7, /device:TPU:25, one launch (start us, length us, event | category | flops | bytes accessed | tf_op | source)
XLA Modules:
  0.0 18.9 jit_solution(8327211383296345028)
XLA Ops:
  0.0 17.9 %shard_map.64 = bf16[128,4096]{1,0:T(8,128)(2,1)S(1)} custom-call(bf16[3,128,4096]{2,1,0:T(8,128)(2,1)} %x_hbm.1, f32[3,3,4096]{2,1,0:T(4,128)} %taps_hbm.1, f32[1,4096]{1,0:T(1,128)} %bitcast.1, f32[2,2,4096]{2,1,0:T(2,128)} %res_hbm.1, f32[2,4096]{1,0:T(2,128)} %ang_hbm.1, f32[2,4096]{1,0:T(2,128)} %dec_hbm.1), custom_call_target="tpu_custom_call" | custom-call | flops 31457280 | bytes 4194304 | tf_op jit(solution)/shard_map/pallas_call | solution.py:490
  17.9 1.0 %copy.8 = bf16[128,4096]{1,0:T(8,128)(2,1)} copy(bf16[128,4096]{1,0:T(8,128)(2,1)S(1)} %shard_map.64) | data formatting | bytes 2097152

commit v8 on v7

--- a/solution.py
+++ b/solution.py
@@ -195,21 +195,21 @@
         for slot, i in enumerate(projections):
             buffer[slot] = jnp.dot(to_chunks[...], xs[i, :, block(b)], preferred_element_type=F32)
 
-    def ordered_blocks(projections, work):
-        order(0, projections, even)
+    def ordered_blocks(projections, work, start, stop):
+        order(start, projections, even)
 
         def two(pair, carry):
-            b = 2 * pair
+            b = start + 2 * pair
             order(b + 1, projections, odd)
             work(b, even)
             order(b + 2, projections, even)
             work(b + 1, odd)
             return carry
 
-        lax.fori_loop(0, blocks // 2 - 1, two, 0)
-        order(blocks - 1, projections, odd)
-        work(blocks - 2, even)
-        work(blocks - 1, odd)
+        lax.fori_loop(0, (stop - start) // 2 - 1, two, 0)
+        order(stop - 1, projections, odd)
+        work(stop - 2, even)
+        work(stop - 1, odd)
 
     def short(i, x, cols, edge):
         at = [x[CHUNKS * r : CHUNKS * (r + 1), :] for r in range(steps)]
@@ -253,7 +253,7 @@
 
     for part in range(kv_parts):
         kv_copy(part).wait()
-    ordered_blocks((1, 2), pass_a)
+    ordered_blocks((1, 2), pass_a, 0, blocks)
 
     pl.when(me > 0)(halo_copy.wait_recv)
     keep = me > 0
@@ -351,7 +351,7 @@
             before = p
         return carry
 
-    ordered_blocks((0,), pass_b)
+    ordered_blocks((0,), pass_b, 0, blocks // 2)
 
     t_in[pl.ds(place, 1)] = t_send[pl.ds(place, 1)]
     for piece in range(pieces):
@@ -375,6 +375,7 @@
         g_copy(group, ahead).start()
 
     in_later_groups(send_g)
+    ordered_blocks((0,), pass_b, blocks // 2, blocks)
 
     gr, gi = wr, wi
     span = 1

time: 19 us -> 19 us (level)
  no operation moved by 1% of the time
where the time goes in v8:
time: 19 us; the launch traced here: 18.9 us
  Pallas kernels  17.9 us (94%)
  local copies, waits for them, and re-layouts  0.97 us (5%)
    pallas_call x1, Pallas kernels, on_device(): pl.pallas_call(functools.partial(kernel, n, members), out_shape=pltpu.VME...  17.9 us
    unnamed x1, local copies, waits for them, and re-layouts  0.97 us

profile of v8, /device:TPU:25, one launch (start us, length us, event | category | flops | bytes accessed | tf_op | source)
XLA Modules:
  0.0 18.9 jit_solution(133150605928406834)
XLA Ops:
  0.0 17.9 %shard_map.64 = bf16[128,4096]{1,0:T(8,128)(2,1)S(1)} custom-call(bf16[3,128,4096]{2,1,0:T(8,128)(2,1)} %x_hbm.1, f32[3,3,4096]{2,1,0:T(4,128)} %taps_hbm.1, f32[1,4096]{1,0:T(1,128)} %bitcast.1, f32[2,2,4096]{2,1,0:T(2,128)} %res_hbm.1, f32[2,4096]{1,0:T(2,128)} %ang_hbm.1, f32[2,4096]{1,0:T(2,128)} %dec_hbm.1), custom_call_target="tpu_custom_call" | custom-call | flops 31457280 | bytes 4194304 | tf_op jit(solution)/shard_map/pallas_call | solution.py:491
  17.9 1.0 %copy.8 = bf16[128,4096]{1,0:T(8,128)(2,1)} copy(bf16[128,4096]{1,0:T(8,128)(2,1)S(1)} %shard_map.64) | data formatting | bytes 2097152
